TPU v7x, 512 devices: a whole 4x4x16 slice. The times are simulated.
512 devices in a mesh: case: 16 (over z_lo, y), space: 32 (over x, z_hi, core).
Axes of the slice: x: 4, y: 4, z: 16 (z_hi: 4, z_lo: 4; z = z_hi * 4 + z_lo), core: 2. Of those that a mesh axis runs over, the one named last changes fastest.
Arguments:
- forcing: bfloat16 [16, 256, 32, 256], P('case', 'space'), may hold values from -3.5 to 3.5
- viscosity: bfloat16 [16, 256, 32, 256], P('case', 'space'), may hold values from 0.099609375 to 1
- measured: bfloat16 [16, 256, 32, 256], P('case', 'space'), may hold values from -1.796875 to 1.796875
- correction: float32 [256, 32, 256], P('space'), may hold values from -6 to 6
- wall_rows: int32 [16, 32], P('case'), may hold values from 0 to 63
Outputs:
- pressure: float32 [16, 256, 32, 256], P('case', 'space')
- gradient: float32 [256, 32, 256], P('space')
All inputs are finite; a program needn't handle non-finite values.
Results may differ from a plain program's by a relative error of at most 0.0003.
Values may be sent and summed in bfloat16 or wider, within the bound.
A program may use at most 64 MiB of HBM per device.

v0:
```python
import math

import jax
import jax.numpy as jnp
from jax import lax
from jax.sharding import PartitionSpec as P


def span_tables(length):
    position = jnp.arange(length, dtype=jnp.int32)
    product = position[:, None] * position[None, :] % length
    radians = product.astype(jnp.float32) * (2.0 * math.pi / length)
    return (jnp.cos(radians), jnp.sin(radians))


def forward_span(field, cosine, sine):
    real_part = jnp.einsum("zxy,zk->kxy", field, cosine, precision=lax.Precision.HIGHEST)
    imag_part = -jnp.einsum("zxy,zk->kxy", field, sine, precision=lax.Precision.HIGHEST)
    return (real_part, imag_part)


def inverse_span(real_part, imag_part, cosine, sine, factor):
    first = jnp.einsum("kxy,kz->zxy", real_part, cosine, precision=lax.Precision.HIGHEST)
    second = jnp.einsum("kxy,kz->zxy", imag_part, sine, precision=lax.Precision.HIGHEST)
    return (first - second) * factor


def wall_bands(wave_number, length, rows, screen_square):
    residue = wave_number % length
    laplace_part = 2.0 - 2.0 * jnp.cos(residue.astype(jnp.float32) * (2.0 * math.pi / length))
    number = wave_number.shape[0]
    middle = jnp.broadcast_to((2.0 + laplace_part + screen_square)[:, None], (number, rows))
    below_band = jnp.concatenate(
        [jnp.zeros((number, 1), jnp.float32), -jnp.ones((number, rows - 1), jnp.float32)], axis=1
    )
    above_band = jnp.concatenate(
        [-jnp.ones((number, rows - 1), jnp.float32), jnp.zeros((number, 1), jnp.float32)], axis=1
    )
    return (below_band, middle, above_band)


def shards(forcing, viscosity, measured, correction, wall_rows):
    span_cells, planes, rows = correction.shape
    spaces = lax.axis_size("space")
    length = span_cells * spaces
    plane_part = planes // spaces
    screen_rate = 1.0 / (2.0 * span_cells)
    factor = screen_rate / length
    cosine, sine = span_tables(length)
    viscous = viscosity[0].astype(jnp.float32)
    walls = wall_rows[0]
    row_index = jnp.arange(rows, dtype=jnp.int32)
    below_band, middle, above_band = wall_bands(
        jnp.arange(length, dtype=jnp.int32), length, rows, screen_rate * screen_rate
    )

    def spectrum_of(field_planes):
        return forward_span(
            lax.all_to_all(field_planes, "space", split_axis=1, concat_axis=0, tiled=True),
            cosine,
            sine,
        )

    def solve_spectrum(parts):
        real_part, imag_part = parts
        stacked = jnp.concatenate([real_part, imag_part], axis=1)
        solved = lax.linalg.tridiagonal_solve(
            below_band, middle, above_band, jnp.swapaxes(stacked, 1, 2)
        )
        solved = jnp.swapaxes(solved, 1, 2)
        return inverse_span(solved[:, :plane_part], solved[:, plane_part:], cosine, sine, factor)

    def back_to_planes(field_span):
        return lax.all_to_all(field_span, "space", split_axis=0, concat_axis=1, tiled=True)

    source_field = forcing[0].astype(jnp.float32) + viscous * correction
    pressure_span = solve_spectrum(spectrum_of(source_field))
    pressure_planes = back_to_planes(pressure_span)
    outside = (row_index[None, None, :] >= walls[None, :, None]).astype(jnp.float32)
    misfit = outside * (pressure_planes - measured[0].astype(jnp.float32))
    adjoint_parts = spectrum_of(misfit)
    adjoint_planes = back_to_planes(solve_spectrum(adjoint_parts))
    case_term = viscous * adjoint_planes
    gradient = lax.psum(case_term, "case")
    return (pressure_planes[None], gradient)


def solution(mesh):
    return jax.shard_map(
        shards,
        mesh=mesh,
        in_specs=(
            P("case", "space", None, None),
            P("case", "space", None, None),
            P("case", "space", None, None),
            P("space", None, None),
            P("case", None),
        ),
        out_specs=(P("case", "space", None, None), P("space", None, None)),
        check_vma=False,
    )
```

profile of v0, /device:TPU:6, one launch (start us, length us, event | category | flops | bytes accessed | tf_op | source)
XLA Modules:
  0.0 367.2 jit_solution(5688196393336202945)
XLA Ops:
  7.2 2.0 fusion.293
  9.2 18.2 %all-to-all-start = ((f32[8,32,256]{2,0,1:T(8,128)}), f32[8,32,256]{2,0,1:T(8,128)S(1)}, u32[]{:S(2)}, u32[]{:S(2)}) async-start(f32[8,32,256]{2,0,1:T(8,128)} %fusion.293), calls=%async_computation | async-start | bytes 524288 | tf_op jit(solution)/shard_map/all_to_all | solution.py:59
  27.5 0.6 copy-done.4
  28.1 18.2 %all-to-all-done = f32[8,32,256]{2,0,1:T(8,128)S(1)} async-done(((f32[8,32,256]{2,0,1:T(8,128)}), f32[8,32,256]{2,0,1:T(8,128)S(1)}, u32[]{:S(2)}, u32[]{:S(2)}) %all-to-all-start) | async-done | bytes 262176 | tf_op jit(solution)/shard_map/all_to_all | solution.py:59
  46.4 1.5 convolution_bitcast_fusion
  47.8 1.5 fusion.292
  49.5 0.8 copy-done.2
  50.5 0.8 slice-done.1
  51.3 10.7 %while.64 = (s32[]{:T(128)}, f32[256]{0:T(256)S(1)}, f32[256,2]{0,1:T(2,128)S(1)}, f32[7,32,256]{2,1,0:T(8,128)S(1)}, f32[7,32,256,2]{2,3,1,0:T(2,128)S(1)}, /*i...) while((s32[]{:T(128)}, f32[256]{0:T(256)S(1)}, ...), condition=%wide.region_1.2_spmd, body=%wide.region_0.1_spmd.sunk | while | flops 98337 | bytes 874457 | solution.py:67
  51.4 0.3 broadcast_divide_fusion.248
  53.0 0.3 broadcast_divide_fusion.248
  54.5 0.3 broadcast_divide_fusion.248
  56.0 0.3 broadcast_divide_fusion.248
  57.6 0.3 broadcast_divide_fusion.248
  59.1 0.3 broadcast_divide_fusion.248
  60.7 0.3 broadcast_divide_fusion.248
  65.0 7.1 %while.65 = (s32[]{:T(128)}, f32[256,2]{0,1:T(2,128)S(1)}, f32[7,32,256,2]{2,3,1,0:T(2,128)S(1)}, f32[7,32,256,2]{2,3,1,0:T(2,128)S(1)}, f32[7,32,256]{2,1,0:T(8...) while((s32[]{:T(128)}, f32[256,2]{0,1:T(2,128)S(1)}, ...), condition=%wide.region_3.4_spmd, body=%wide.region_2.3_spmd.sunk | while | flops 48161 | bytes 510029 | solution.py:67
  65.2 0.2 constant_dynamic-update-slice_fusion.416
  66.2 0.2 constant_dynamic-update-slice_fusion.416
  67.2 0.2 constant_dynamic-update-slice_fusion.416
  68.2 0.2 constant_dynamic-update-slice_fusion.416
  70.2 0.2 constant_dynamic-update-slice_fusion.416
  71.2 0.2 constant_dynamic-update-slice_fusion.416
  72.9 0.2 maximum_bitcast_fusion.1
  73.1 0.4 fusion.675
  73.5 1.5 fusion.305
  75.1 1.5 fusion.291
  76.6 1.0 copy.114
  77.6 7.5 %all-to-all-start.1 = ((f32[256,1,256]{2,1,0:T(1,128)}), f32[256,1,256]{2,1,0:T(1,128)S(1)}, u32[]{:S(2)}, u32[]{:S(2)}) async-start(f32[256,1,256]{2,1,0:T(1,128)} %copy.114), calls=%async_computation.1 | async-start | bytes 524288 | tf_op jit(solution)/shard_map/all_to_all | solution.py:74
  85.1 0.6 copy-done.8
  85.9 17.5 %all-to-all-done.1 = f32[256,1,256]{2,1,0:T(1,128)S(1)} async-done(((f32[256,1,256]{2,1,0:T(1,128)}), f32[256,1,256]{2,1,0:T(1,128)S(1)}, u32[]{:S(2)}, u32[]{:S(2)}) %all-to-all-start.1) | async-done | bytes 262176 | tf_op jit(solution)/shard_map/all_to_all | solution.py:74
  103.4 0.8 fusion.297
  104.2 8.1 %all-to-all-start.2 = ((f32[8,32,256]{2,0,1:T(8,128)}), f32[8,32,256]{2,0,1:T(8,128)S(1)}, u32[]{:S(2)}, u32[]{:S(2)}) async-start(f32[8,32,256]{2,0,1:T(8,128)} %fusion.297), calls=%async_computation.2 | async-start | bytes 524288 | tf_op jit(solution)/shard_map/all_to_all | solution.py:59
  112.3 18.0 %all-to-all-done.2 = f32[8,32,256]{2,0,1:T(8,128)S(1)} async-done(((f32[8,32,256]{2,0,1:T(8,128)}), f32[8,32,256]{2,0,1:T(8,128)S(1)}, u32[]{:S(2)}, u32[]{:S(2)}) %all-to-all-start.2) | async-done | bytes 262176 | tf_op jit(solution)/shard_map/all_to_all | solution.py:59
  130.3 1.5 fusion.309
  132.0 1.5 convolution_negate_fusion
  133.7 0.5 maximum_bitcast_fusion.2
  134.4 0.8 copy-done
  135.3 0.9 slice-done
  136.2 11.0 %while.66 = (s32[]{:T(128)}, f32[256]{0:T(256)S(1)}, f32[256,2]{0,1:T(2,128)S(1)}, f32[7,32,256]{2,1,0:T(8,128)S(1)}, f32[7,32,256,2]{2,3,1,0:T(2,128)S(1)}, /*i...) while((s32[]{:T(128)}, f32[256]{0:T(256)S(1)}, ...), condition=%wide.region_5.6_spmd, body=%wide.region_4.5_spmd.sunk | while | flops 99873 | bytes 746641 | solution.py:67
  136.3 0.3 broadcast_divide_fusion.249
  137.9 0.3 broadcast_divide_fusion.249
  139.5 0.3 broadcast_divide_fusion.249
  141.1 0.3 broadcast_divide_fusion.249
  142.6 0.3 broadcast_divide_fusion.249
  144.2 0.3 broadcast_divide_fusion.249
  145.8 0.3 broadcast_divide_fusion.249
  149.3 0.9 copy-done.1
  151.1 7.0 %while.67 = (s32[]{:T(128)}, f32[256,2]{0,1:T(2,128)S(1)}, f32[7,32,256,2]{2,3,1,0:T(2,128)S(1)}, f32[7,32,256,2]{2,3,1,0:T(2,128)S(1)}, f32[7,32,256]{2,1,0:T(8...) while((s32[]{:T(128)}, f32[256,2]{0,1:T(2,128)S(1)}, ...), condition=%wide.region_7.8_spmd, body=%wide.region_6.7_spmd.sunk | while | flops 48161 | bytes 510029 | solution.py:67
  151.3 0.2 constant_dynamic-update-slice_fusion.480
  152.3 0.2 constant_dynamic-update-slice_fusion.480
  153.3 0.2 constant_dynamic-update-slice_fusion.480
  155.3 0.2 constant_dynamic-update-slice_fusion.480
  156.3 0.2 constant_dynamic-update-slice_fusion.480
  158.8 0.2 maximum_bitcast_fusion.3
  159.0 0.4 fusion.674
  159.4 1.5 fusion.300
  160.9 1.5 fusion.289
  162.5 0.3 copy.116
  162.8 26.9 %all_to_all.66 = f32[256,1,256]{2,1,0:T(1,128)S(1)} all-to-all(f32[256,1,256]{2,1,0:T(1,128)S(1)} %copy.116), channel_id=1, replica_groups=mesh['case'=16,'space'=32] {'space'}, dimensions={0} | all-to-all | bytes 524288 | tf_op jit(solution)/shard_map/all_to_all | solution.py:74
  189.6 0.8 convert_multiply_fusion
  190.5 0.8 copy.117
  191.3 167.4 %all-reduce.2.cloned.1.call-done = f32[8,32,256]{2,0,1:T(8,128)} async-done(((f32[8,32,256]{2,0,1:T(8,128)}), f32[8,32,256]{2,0,1:T(8,128)}) %all-reduce.2.cloned.1.call-update) | async-done | bytes 262160 | tf_op jit(solution)/shard_map/psum | solution.py:84
  358.6 1.7 copy.118
  (1293 shorter events, 32.4 us)
Async XLA Ops:
  9.2 37.1 %all-to-all-start = ((f32[8,32,256]{2,0,1:T(8,128)}), f32[8,32,256]{2,0,1:T(8,128)S(1)}, u32[]{:S(2)}, u32[]{:S(2)}) async-start(f32[8,32,256]{2,0,1:T(8,128)} %fusion.293), calls=%async_computation | async-start | bytes 524288 | tf_op jit(solution)/shard_map/all_to_all | solution.py:59
  27.5 0.6 copy-start.4
  49.4 0.8 copy-start.2
  50.3 1.0 slice-start.1
  50.4 0.9 copy-start.6
  77.6 25.8 %copy-start.7 = (bf16[1,8,32,256]{3,2,1,0:T(8,128)(2,1)S(1)}, bf16[1,8,32,256]{3,2,1,0:T(8,128)(2,1)}, u32[]{:S(2)}) copy-start(bf16[1,8,32,256]{3,2,1,0:T(8,128)(2,1)} %param.15) | copy-start | bytes 393220
  77.6 25.8 %all-to-all-start.1 = ((f32[256,1,256]{2,1,0:T(1,128)}), f32[256,1,256]{2,1,0:T(1,128)S(1)}, u32[]{:S(2)}, u32[]{:S(2)}) async-start(f32[256,1,256]{2,1,0:T(1,128)} %copy.114), calls=%async_computation.1 | async-start | bytes 524288 | tf_op jit(solution)/shard_map/all_to_all | solution.py:74
  85.1 0.7 copy-start.8
  104.2 26.1 %all-to-all-start.2 = ((f32[8,32,256]{2,0,1:T(8,128)}), f32[8,32,256]{2,0,1:T(8,128)S(1)}, u32[]{:S(2)}, u32[]{:S(2)}) async-start(f32[8,32,256]{2,0,1:T(8,128)} %fusion.297), calls=%async_computation.2 | async-start | bytes 524288 | tf_op jit(solution)/shard_map/all_to_all | solution.py:59
  112.3 246.4 %all-reduce.2.cloned.1.call-start = ((), (), s32[]{:S(2)}) async-start(), calls=%async_computation.4 | async-start | bytes 524288 | tf_op jit(solution)/shard_map/psum | solution.py:84
  134.3 0.8 copy-start
  135.1 1.0 slice-start
  135.3 0.9 copy-start.5
  149.1 1.0 copy-start.1
  162.7 26.9 %copy-start.3 = (bf16[1,8,32,256]{3,2,1,0:T(8,128)(2,1)S(1)}, bf16[1,8,32,256]{3,2,1,0:T(8,128)(2,1)}, u32[]{:S(2)}) copy-start(bf16[1,8,32,256]{3,2,1,0:T(8,128)(2,1)} %param.14) | copy-start | bytes 393220
Sparse Core Ops, SparseCore 0:
  190.6 168.0 all-reduce.1
where the time goes:
time: 368 us; the launch traced here: 367 us
  waiting for transfers between devices  221 us (60%)
  starting transfers between devices  33.9 us (9%)
  other arithmetic  29.4 us (8%)
  blocking collectives  26.9 us (7%)
  local copies, waits for them, and re-layouts  24 us (7%)
  between operations  15.3 us (4%)
  matrix products  12 us (3%)
  loops' own time  4.56 us (1%)
    psum x1, waiting for transfers between devices, shards(): gradient = lax.psum(case_term, 'case')  167 us
    all_to_all x2, waiting for transfers between devices, spectrum_of(): lax.all_to_all(field_planes, 'space', split_axis=1, concat_axis=0, tiled=...  36.2 us
    all_to_all x1, blocking collectives, back_to_planes(): lax.all_to_all(field_span, 'space', split_axis=0, concat_axis=1, tiled=True)  26.9 us
    all_to_all x2, starting transfers between devices, spectrum_of(): lax.all_to_all(field_planes, 'space', split_axis=1, concat_axis=0, tiled=...  26.3 us
    all_to_all x1, waiting for transfers between devices, back_to_planes(): lax.all_to_all(field_span, 'space', split_axis=0, concat_axis=1, tiled=True)  17.5 us
    while x630, other arithmetic  14.8 us
    slice x85, local copies, waits for them, and re-layouts, solve_spectrum(): lax.linalg.tridiagonal_solve(below_band, middle, above_band, jnp.swapaxes...  9.17 us
    all_to_all x1, starting transfers between devices, back_to_planes(): lax.all_to_all(field_span, 'space', split_axis=0, concat_axis=1, tiled=True)  7.55 us
  transfers between devices with their start and end apart: 4, of which 4 were waited for; matrix products, arithmetic and copies ran while one was open for 0% of the time, Pallas kernels for 0%

commit v1 on v0

v1 whole, which is shorter than its diff:
```python
import functools

import jax
import jax.numpy as jnp
import ml_dtypes
import numpy as np
from jax import lax
from jax.experimental import pallas as pl
from jax.experimental.pallas import tpu as pltpu
from jax.sharding import PartitionSpec as P

MESH = pl.DeviceIdType.MESH
F32, BF16 = jnp.float32, jnp.bfloat16


def sine_tables(rows):
    index = np.arange(1, rows + 1, dtype=np.float64)
    phase = (index[:, None] * index[None, :]) % (2 * (rows + 1))
    sine = np.sqrt(2.0 / (rows + 1)) * np.sin(np.pi * phase / (rows + 1))
    high = sine.astype(ml_dtypes.bfloat16)
    low = (sine - high.astype(np.float64)).astype(ml_dtypes.bfloat16)
    return high, low


def mode_table(rows, cells, length, screen):
    index = np.arange(1, rows + 1, dtype=np.float64)
    centre = 4.0 * np.sin(np.pi * index / (2 * (rows + 1))) ** 2 + screen * screen
    rate = 1.0 + centre / 2.0 - np.sqrt(centre + centre * centre / 4.0)
    blocks = length // cells
    lines = [rate, 1.0 / (1.0 - rate**length), screen / (1.0 / rate - rate)]
    step = 1
    while step < blocks:
        lines.append(rate ** (cells * step))
        step *= 2
    table = np.zeros((-(-len(lines) // 8) * 8, rows))
    table[: len(lines)] = lines
    return table.astype(np.float32)


def wait_bytes(ref, sem):
    pltpu.make_async_copy(ref, ref, sem).wait()


def kernel(spaces, cases, cells, planes, rows, forcing, viscosity, measured, correction, walls, high_ref, low_ref, modes,
           pressure_out, gradient_out, head, tail, spectrum, result, send1, got1, send2, got2, send3, got3, send4, got4,
           part_got, part_sum, sems, out_sem):
    me = lax.axis_index("space")
    case = lax.axis_index("case")
    lanes = 128
    groups = rows // lanes
    part = cells * planes // cases

    barrier = pltpu.get_barrier_semaphore()

    def greet(axis, mine, count):
        def one(k, carry):
            pl.semaphore_signal(barrier, inc=1, device_id={axis: lax.rem(mine + k, count)}, device_id_type=MESH)
            return carry

        lax.fori_loop(1, count, one, 0)

    greet("space", me, spaces)
    greet("case", case, cases)

    rate = modes[0:1, :]
    around = modes[1:2, :]
    scale = modes[2:3, :]

    def split(i, value):
        top = value.astype(BF16)
        head[i * planes : (i + 1) * planes, :] = top
        tail[i * planes : (i + 1) * planes, :] = (value - top.astype(F32)).astype(BF16)

    def sine():
        high, low = high_ref[...], low_ref[...]
        top = head[...]
        small = jnp.dot(top, low, preferred_element_type=F32) + jnp.dot(tail[...], high, preferred_element_type=F32)
        return jnp.dot(top, high, preferred_element_type=F32) + small

    def at(ref, i):
        return ref[i * planes : (i + 1) * planes, :]

    def exchange(send, got, phase):
        def one(k, carry):
            other = lax.rem(me + k, spaces)
            pltpu.make_async_remote_copy(
                src_ref=send.at[other],
                dst_ref=got.at[me],
                send_sem=sems.at[2 * phase],
                recv_sem=sems.at[2 * phase + 1],
                device_id={"space": other},
                device_id_type=MESH,
            ).start()
            return carry

        lax.fori_loop(1, spaces, one, 0)
        got[pl.ds(me, 1)] = send[pl.ds(me, 1)]

    def arrived(got, phase):
        wait_bytes(got.at[pl.ds(0, spaces - 1)], sems.at[2 * phase + 1])

    def sent(send, phase):
        wait_bytes(send.at[pl.ds(0, spaces - 1)], sems.at[2 * phase])

    def put(ref, first, second):
        for g in range(groups):
            ref[:, g, :] = first[:, g * lanes : (g + 1) * lanes]
            ref[:, groups + g, :] = second[:, g * lanes : (g + 1) * lanes]

    def take(ref):
        first = jnp.concatenate([ref[:, g, :] for g in range(groups)], axis=1)
        second = jnp.concatenate([ref[:, groups + g, :] for g in range(groups)], axis=1)
        return first, second

    def solve(send_a, got_a, send_b, got_b, phase, before_send=None):
        spectrum[...] = sine()
        onward = rate * at(spectrum, 0)
        backward = rate * at(spectrum, cells - 1)
        for i in range(1, cells):
            onward = (onward + at(spectrum, i)) * rate
            backward = (backward + at(spectrum, cells - 1 - i)) * rate
        put(send_a, onward, backward)
        if before_send is not None:
            before_send()
        exchange(send_a, got_a, phase)
        arrived(got_a, phase)
        onward, backward = take(got_a)
        step, line = 1, 3
        while step < spaces:
            power = modes[line : line + 1, :]
            onward = onward + power * pltpu.roll(onward, step, 0)
            backward = backward + power * pltpu.roll(backward, spaces - step, 0)
            step, line = 2 * step, line + 1
        put(send_b, pltpu.roll(onward, 1, 0) * around, pltpu.roll(backward, spaces - 1, 0) * around)
        exchange(send_b, got_b, phase + 1)
        arrived(got_b, phase + 1)
        left, right = take(got_b)
        running = right
        for i in range(cells - 1, -1, -1):
            at_i = at(spectrum, i)
            result[i * planes : (i + 1) * planes, :] = running
            running = (running + at_i) * rate
        running = left
        for i in range(cells):
            running = at(spectrum, i) + (running if i == 0 else running * rate)
            split(i, (running + at(result, i)) * scale)
        result[...] = sine()

    for i in range(cells):
        split(i, at(forcing, i).astype(F32) + at(viscosity, i).astype(F32) * at(correction, i))

    solve(send1, got1, send2, got2, 0, lambda: pl.semaphore_wait(barrier, spaces + cases - 2))

    pressure = spectrum
    sent(send1, 0)
    sent(send2, 1)
    diagonal = lax.broadcasted_iota(jnp.int32, (planes, planes), 0) == lax.broadcasted_iota(
        jnp.int32, (planes, planes), 1
    )
    first_row = jnp.sum(jnp.where(diagonal, walls[...], 0), axis=1, keepdims=True)
    outside = lax.broadcasted_iota(jnp.int32, (planes, rows), 1) >= first_row
    copy_out = pltpu.make_async_copy(part_sum, pressure_out, out_sem)
    for i in range(cells):
        value = at(result, i)
        part_sum[i * planes : (i + 1) * planes, :] = value
        split(i, jnp.where(outside, value - at(measured, i).astype(F32), 0.0))
    copy_out.start()
    solve(send3, got3, send4, got4, 2)
    sent(send3, 2)
    sent(send4, 3)
    copy_out.wait()
    for i in range(cells):
        result[i * planes : (i + 1) * planes, :] = at(viscosity, i).astype(F32) * at(result, i)

    def to_case(k, carry):
        other = lax.rem(case + k, cases)
        pltpu.make_async_remote_copy(
            src_ref=result.at[pl.ds(pl.multiple_of(other * part, part), part)],
            dst_ref=part_got.at[case],
            send_sem=sems.at[8],
            recv_sem=sems.at[9],
            device_id={"case": other},
            device_id_type=MESH,
        ).start()
        return carry

    lax.fori_loop(1, cases, to_case, 0)
    mine = pl.ds(pl.multiple_of(case * part, part), part)
    part_got[case] = result[mine]
    wait_bytes(part_got.at[pl.ds(0, cases - 1)], sems.at[9])
    total = part_got[0]
    for k in range(1, cases):
        total = total + part_got[k]
    part_sum[0:part, :] = total

    def to_all(k, carry):
        other = lax.rem(case + k, cases)
        pltpu.make_async_remote_copy(
            src_ref=part_sum.at[0:part],
            dst_ref=gradient_out.at[mine],
            send_sem=sems.at[10],
            recv_sem=sems.at[11],
            device_id={"case": other},
            device_id_type=MESH,
        ).start()
        return carry

    lax.fori_loop(1, cases, to_all, 0)
    keep = pltpu.make_async_copy(part_sum.at[0:part], gradient_out.at[mine], out_sem)
    keep.start()
    keep.wait()
    wait_bytes(gradient_out.at[pl.ds(0, (cases - 1) * part)], sems.at[11])
    wait_bytes(result.at[pl.ds(0, (cases - 1) * part)], sems.at[8])
    wait_bytes(result.at[pl.ds(0, (cases - 1) * part)], sems.at[10])


def shards(forcing, viscosity, measured, correction, wall_rows):
    cells, planes, rows = correction.shape
    spaces, cases = lax.axis_size("space"), lax.axis_size("case")
    length = cells * spaces
    high, low = sine_tables(rows)
    modes = mode_table(rows, cells, length, 1.0 / (2.0 * cells))
    flat = (cells * planes, rows)
    part = cells * planes // cases
    exchanged = [pltpu.VMEM((spaces, 2 * rows // 128, 128), F32)] * 8
    vmem = pl.BlockSpec(memory_space=pltpu.VMEM)
    pressure, gradient = pl.pallas_call(
        functools.partial(kernel, spaces, cases, cells, planes, rows),
        out_shape=(jax.ShapeDtypeStruct(flat, F32), jax.ShapeDtypeStruct(flat, F32)),
        in_specs=[vmem] * 8,
        out_specs=(pl.BlockSpec(memory_space=pl.ANY),) * 2,
        scratch_shapes=[
            pltpu.VMEM(flat, BF16),
            pltpu.VMEM(flat, BF16),
            pltpu.VMEM(flat, F32),
            pltpu.VMEM(flat, F32),
            *exchanged,
            pltpu.VMEM((cases, part, rows), F32),
            pltpu.VMEM(flat, F32),
            pltpu.SemaphoreType.DMA((12,)),
            pltpu.SemaphoreType.DMA,
        ],
        compiler_params=pltpu.CompilerParams(
            collective_id=0, has_side_effects=True, vmem_limit_bytes=16 * 1024 * 1024
        ),
    )(
        forcing.reshape(flat),
        viscosity.reshape(flat),
        measured.reshape(flat),
        correction.reshape(flat),
        wall_rows,
        jnp.asarray(high),
        jnp.asarray(low),
        jnp.asarray(modes),
    )
    return pressure.reshape(forcing.shape), gradient.reshape(correction.shape)


def solution(mesh):
    return jax.shard_map(
        shards,
        mesh=mesh,
        in_specs=(
            P("case", "space", None, None),
            P("case", "space", None, None),
            P("case", "space", None, None),
            P("space", None, None),
            P("case", None),
        ),
        out_specs=(P("case", "space", None, None), P("space", None, None)),
        check_vma=False,
    )
```

time: 368 us -> 78.1 us (0.21)
  the two profiles are of different devices: /device:TPU:6 before, /device:TPU:1 now
where the time goes in v1:
time: 78.1 us; the launch traced here: 77.3 us
  Pallas kernels  69.1 us (88%)
  local copies, waits for them, and re-layouts  7.56 us (10%)
    pallas_call x1, Pallas kernels, shards(): pl.pallas_call(functools.partial(kernel, spaces, cases, cells, planes, ro...  69.1 us
    unnamed x18, local copies, waits for them, and re-layouts  7.56 us

profile of v1, /device:TPU:1, one launch (start us, length us, event | category | flops | bytes accessed | tf_op | source)
XLA Modules:
  0.0 77.3 jit_solution(9180797592899605345)
XLA Ops:
  0.6 0.0 copy-start.6
  0.6 0.0 copy-start.7
  0.7 0.7 copy-done.6
  1.3 0.0 copy-done.7
  1.3 0.0 copy-start
  1.3 0.9 %copy-done = f32[8,32,256]{2,1,0:T(8,128)S(1)} copy-done((f32[8,32,256]{2,1,0:T(8,128)S(1)}, f32[8,32,256]{2,1,0:T(8,128)}, u32[]{:S(2)}) %copy-start) | copy-done | bytes 262168
  2.3 0.0 copy-start.1
  2.3 0.9 %copy-done.1 = bf16[1,8,32,256]{3,2,1,0:T(8,128)(2,1)S(1)} copy-done((bf16[1,8,32,256]{3,2,1,0:T(8,128)(2,1)S(1)}, bf16[1,8,32,256]{3,2,1,0:T(8,128)(2,1)}, u32[]{:S(2)}) %copy-start.1) | copy-done | bytes 131096
  3.2 0.0 copy-start.2
  3.2 0.9 %copy-done.2 = bf16[1,8,32,256]{3,2,1,0:T(8,128)(2,1)S(1)} copy-done((bf16[1,8,32,256]{3,2,1,0:T(8,128)(2,1)S(1)}, bf16[1,8,32,256]{3,2,1,0:T(8,128)(2,1)}, u32[]{:S(2)}) %copy-start.2) | copy-done | bytes 131096
  4.1 0.0 copy-start.3
  4.1 0.9 %copy-done.3 = bf16[1,8,32,256]{3,2,1,0:T(8,128)(2,1)S(1)} copy-done((bf16[1,8,32,256]{3,2,1,0:T(8,128)(2,1)S(1)}, bf16[1,8,32,256]{3,2,1,0:T(8,128)(2,1)}, u32[]{:S(2)}) %copy-start.3) | copy-done | bytes 131096
  5.0 0.0 copy-start.4
  5.0 0.9 %copy-done.4 = bf16[256,256]{1,0:T(8,128)(2,1)S(1)} copy-done((bf16[256,256]{1,0:T(8,128)(2,1)S(1)}, bf16[256,256]{1,0:T(8,128)(2,1)}, u32[]{:S(2)}) %copy-start.4) | copy-done | bytes 131096
  5.9 0.0 copy-start.5
  5.9 0.9 %copy-done.5 = bf16[256,256]{1,0:T(8,128)(2,1)S(1)} copy-done((bf16[256,256]{1,0:T(8,128)(2,1)S(1)}, bf16[256,256]{1,0:T(8,128)(2,1)}, u32[]{:S(2)}) %copy-start.5) | copy-done | bytes 131096
  6.8 69.1 %shard_map.95 = (f32[256,256]{1,0:T(8,128)S(1)}, f32[256,256]{1,0:T(8,128)S(1)}) custom-call(bf16[256,256]{1,0:T(8,128)(2,1)S(1)} %bitcast.9, bf16[256,256]{1,0:T(8,128)(2,1)S(1)} %bitcast.10, bf16[256,256]{1,0:T(8,128)(2,1)S(1)} %bitcast.11, f32[256,256]{1,0:T(8,128)S(1)} %bitcast.6, s32[1,32]{1,0:T(1,128)S(1)} %copy-done.7, ...), custom_call_target="tpu_custom_call" | custom-call | tf_op jit(solution)/shard_map/pallas_call | solution.py:227
  75.9 0.7 copy.12
  76.6 0.7 copy.13
Async XLA Ops:
  0.6 0.7 copy-start.6
  0.6 0.7 copy-start.7
  1.3 1.0 %copy-start = (f32[8,32,256]{2,1,0:T(8,128)S(1)}, f32[8,32,256]{2,1,0:T(8,128)}, u32[]{:S(2)}) copy-start(f32[8,32,256]{2,1,0:T(8,128)} %param.11) | copy-start | bytes 786436
  2.3 0.9 %copy-start.1 = (bf16[1,8,32,256]{3,2,1,0:T(8,128)(2,1)S(1)}, bf16[1,8,32,256]{3,2,1,0:T(8,128)(2,1)}, u32[]{:S(2)}) copy-start(bf16[1,8,32,256]{3,2,1,0:T(8,128)(2,1)} %param.8) | copy-start | bytes 393220
  3.2 0.9 %copy-start.2 = (bf16[1,8,32,256]{3,2,1,0:T(8,128)(2,1)S(1)}, bf16[1,8,32,256]{3,2,1,0:T(8,128)(2,1)}, u32[]{:S(2)}) copy-start(bf16[1,8,32,256]{3,2,1,0:T(8,128)(2,1)} %param.9) | copy-start | bytes 393220
  4.1 0.9 %copy-start.3 = (bf16[1,8,32,256]{3,2,1,0:T(8,128)(2,1)S(1)}, bf16[1,8,32,256]{3,2,1,0:T(8,128)(2,1)}, u32[]{:S(2)}) copy-start(bf16[1,8,32,256]{3,2,1,0:T(8,128)(2,1)} %param.10) | copy-start | bytes 393220
  5.0 0.9 %copy-start.4 = (bf16[256,256]{1,0:T(8,128)(2,1)S(1)}, bf16[256,256]{1,0:T(8,128)(2,1)}, u32[]{:S(2)}) copy-start(bf16[256,256]{1,0:T(8,128)(2,1)} %constant.7.clone.low_ref) | copy-start | bytes 393220
  5.9 0.9 %copy-start.5 = (bf16[256,256]{1,0:T(8,128)(2,1)S(1)}, bf16[256,256]{1,0:T(8,128)(2,1)}, u32[]{:S(2)}) copy-start(bf16[256,256]{1,0:T(8,128)(2,1)} %constant.6.clone.high_ref) | copy-start | bytes 393220

commit v2 on v1

v2 whole, which is shorter than its diff:
```python
import functools

import jax
import jax.numpy as jnp
import ml_dtypes
import numpy as np
from jax import lax
from jax.experimental import pallas as pl
from jax.experimental.pallas import tpu as pltpu
from jax.sharding import PartitionSpec as P

MESH = pl.DeviceIdType.MESH
F32, BF16, I32 = jnp.float32, jnp.bfloat16, jnp.int32
OUTER, MIDDLE = 4, 4
TOP = 32767.0


def sine_tables(rows):
    index = np.arange(1, rows + 1, dtype=np.float64)
    phase = (index[:, None] * index[None, :]) % (2 * (rows + 1))
    sine = np.sqrt(2.0 / (rows + 1)) * np.sin(np.pi * phase / (rows + 1))
    high = sine.astype(ml_dtypes.bfloat16)
    low = (sine - high.astype(np.float64)).astype(ml_dtypes.bfloat16)
    return high, low


def mode_table(rows, cells, length, screen):
    index = np.arange(1, rows + 1, dtype=np.float64)
    centre = 4.0 * np.sin(np.pi * index / (2 * (rows + 1))) ** 2 + screen * screen
    rate = 1.0 + centre / 2.0 - np.sqrt(centre + centre * centre / 4.0)
    block = rate**cells
    lines = [
        rate,
        block,
        block**2,
        block ** (2 * MIDDLE),
        block ** (2 * MIDDLE * (OUTER - 1)),
        1.0 / (1.0 - rate**length),
        screen / (1.0 / rate - rate),
        np.zeros(rows),
    ]
    return np.stack(lines).astype(np.float32)


def wait_bytes(ref, sem):
    pltpu.make_async_copy(ref, ref, sem).wait()


def pack(ref, first, second):
    count = first.shape[0]
    largest = jnp.max(jnp.maximum(jnp.abs(first), jnp.abs(second)), axis=0, keepdims=True)
    code = jnp.ceil(jnp.log2(jnp.maximum(largest, 1e-30)) * 64.0)
    factor = TOP * jnp.exp2(code * (-1.0 / 64.0))
    a = jnp.round(first * factor).astype(I32)
    b = jnp.round(second * factor).astype(I32)
    ref[0:count, :] = (a << 16) | (b & 0xFFFF)
    ref[count : count + 1, :] = code.astype(I32)


def unpack(ref):
    count = ref.shape[0] - 1
    scale = jnp.exp2(ref[count : count + 1, :].astype(F32) * (1.0 / 64.0)) * (1.0 / TOP)
    words = ref[0:count, :]
    return (words >> 16).astype(F32) * scale, ((words << 16) >> 16).astype(F32) * scale


def kernel(cases, cells, planes, rows, forcing_in, viscosity_in, measured_in, correction_in, walls_in, high_in, low_in,
           modes_in, pressure_out, gradient_out, forcing, viscosity, measured, correction, walls, high_ref, low_ref, modes,
           head, tail, spectrum, result, moments, pressure, xs_send, xs_got, hs_send, hs_got, cs_send, cs_got,
           rs_send, rs_got, ag_send, ag_got, in_sems, out_sems, sends, recvs):
    me = lax.axis_index("space")
    case = lax.axis_index("case")
    inner, middle, outer = me % 2, me // 2 % MIDDLE, me // (2 * MIDDLE)
    half = planes // 2
    part = cells * planes // cases

    def space(o, m, i):
        return {"space": (o * MIDDLE + m) * 2 + i}

    barrier = pltpu.get_barrier_semaphore()

    def greet(device):
        pl.semaphore_signal(barrier, inc=1, device_id=device, device_id_type=MESH)

    for k in (2, 1, 3):
        greet(space(outer, (middle + k) % MIDDLE, inner))
    loads = [
        pltpu.make_async_copy(src, dst, in_sems.at[i])
        for i, (src, dst) in enumerate(
            (
                (forcing_in, forcing),
                (viscosity_in, viscosity),
                (correction_in, correction),
                (high_in, high_ref),
                (low_in, low_ref),
                (modes_in, modes),
                (walls_in, walls),
                (measured_in, measured),
            )
        )
    ]
    for load in loads:
        load.start()
    for k in range(1, cases):
        greet({"case": (case + k) % cases})
    for k in range(1, 2 * OUTER):
        greet(space((outer + k // 2) % OUTER, middle, (inner + k) % 2))

    def at(ref, i):
        return ref[i * planes : (i + 1) * planes, :]

    def split(i, value):
        top = value.astype(BF16)
        head[i * planes : (i + 1) * planes, :] = top
        tail[i * planes : (i + 1) * planes, :] = (value - top.astype(F32)).astype(BF16)

    def sine():
        high, low = high_ref[...], low_ref[...]
        top = head[...]
        small = jnp.dot(top, low, preferred_element_type=F32) + jnp.dot(tail[...], high, preferred_element_type=F32)
        return jnp.dot(top, high, preferred_element_type=F32) + small

    def line(i):
        return modes[i : i + 1, :]

    def send(src, dst, phase, device):
        pltpu.make_async_remote_copy(
            src_ref=src, dst_ref=dst, send_sem=sends.at[phase], recv_sem=recvs.at[phase], device_id=device, device_id_type=MESH
        ).start()

    def solve(turn, before_send=None):
        first = 3 * turn
        spectrum[...] = sine()
        rate = line(0)
        onward = rate * at(spectrum, 0)
        backward = rate * at(spectrum, cells - 1)
        for i in range(1, cells):
            onward = (onward + at(spectrum, i)) * rate
            backward = (backward + at(spectrum, cells - 1 - i)) * rate
        for i in range(2):
            moments[0, i] = onward[i * half : (i + 1) * half]
            moments[1, i] = backward[i * half : (i + 1) * half]
            pack(xs_send.at[turn, i], moments[0, i], moments[1, i])
        if before_send is not None:
            before_send()
        for k in (4, 5, 2, 3, 6, 7, 1):
            to_inner = (inner + k) % 2
            send(
                xs_send.at[turn, to_inner],
                xs_got.at[turn, 2 * outer + inner],
                first,
                space((outer + k // 2) % OUTER, middle, to_inner),
            )
        wait_bytes(xs_got.at[turn, pl.ds(0, 2 * OUTER - 1)], recvs.at[first])

        block, two, eight, most = line(1), line(2), line(3), line(4)
        own_l, own_r = moments[0, inner], moments[1, inner]
        other_l, other_r = unpack(xs_got.at[turn, 2 * outer + 1 - inner])
        is_first = inner == 0
        l0, l1 = jnp.where(is_first, own_l, other_l), jnp.where(is_first, other_l, own_l)
        r0, r1 = jnp.where(is_first, own_r, other_r), jnp.where(is_first, other_r, own_r)
        chip_l, chip_r = l0 * block + l1, r0 + r1 * block
        pairs = []
        for d in range(1, OUTER):
            slot = 2 * ((outer + d) % OUTER)
            a_l, a_r = unpack(xs_got.at[turn, slot])
            b_l, b_r = unpack(xs_got.at[turn, slot + 1])
            pairs.append((a_l * block + b_l, a_r + b_r * block))
        before = pairs[0][0]
        after = pairs[OUTER - 2][1]
        for d in range(1, OUTER - 1):
            before = pairs[d][0] + eight * before
            after = pairs[OUTER - 2 - d][1] + eight * after
        onto, round_l = chip_l + eight * before, before + most * chip_l
        back, round_r = chip_r + eight * after, after + most * chip_r
        pack(hs_send.at[turn, 0], onto, round_r)
        pack(hs_send.at[turn, 1], round_l, back)
        for k in (2, 1, 3):
            send(
                hs_send.at[turn, (middle + k) // MIDDLE],
                hs_got.at[turn, middle],
                first + 1,
                space(outer, (middle + k) % MIDDLE, inner),
            )
        wait_bytes(hs_got.at[turn, pl.ds(0, MIDDLE - 1)], recvs.at[first + 1])
        near = [unpack(hs_got.at[turn, (middle + d) % MIDDLE]) for d in range(1, MIDDLE)]
        left, right = round_l, round_r
        for d in range(1, MIDDLE):
            left = near[d - 1][0] + two * left
            right = near[MIDDLE - 1 - d][1] + two * right
        left, right = left * line(5), right * line(5)
        left_1, right_0 = left * block + l0, right * block + r1
        cs_send[turn, 0] = jnp.where(is_first, left_1, left)
        cs_send[turn, 1] = jnp.where(is_first, right, right_0)
        send(cs_send.at[turn], cs_got.at[turn, inner], first + 2, space(outer, middle, 1 - inner))
        cs_got[turn, inner, 0] = jnp.where(is_first, left, left_1)
        cs_got[turn, inner, 1] = jnp.where(is_first, right_0, right)
        wait_bytes(cs_got.at[turn, 0], recvs.at[first + 2])

        left = jnp.concatenate([cs_got[turn, 0, 0], cs_got[turn, 1, 0]], axis=0)
        right = jnp.concatenate([cs_got[turn, 0, 1], cs_got[turn, 1, 1]], axis=0)
        running = right
        for i in range(cells - 1, -1, -1):
            result[i * planes : (i + 1) * planes, :] = running
            running = (running + at(spectrum, i)) * rate
        running = left
        for i in range(cells):
            running = at(spectrum, i) + (running if i == 0 else running * rate)
            split(i, (running + at(result, i)) * line(6))
        result[...] = sine()

    for i in range(3):
        loads[i].wait()
    for i in range(cells):
        split(i, at(forcing, i).astype(F32) + at(viscosity, i).astype(F32) * at(correction, i))
    for i in range(3, 8):
        loads[i].wait()

    solve(0, lambda: pl.semaphore_wait(barrier, cases - 1 + MIDDLE - 1 + 2 * OUTER - 1))

    diagonal = lax.broadcasted_iota(I32, (planes, planes), 0) == lax.broadcasted_iota(I32, (planes, planes), 1)
    first_row = jnp.sum(jnp.where(diagonal, walls[...], 0), axis=1, keepdims=True)
    outside = lax.broadcasted_iota(I32, (planes, rows), 1) >= first_row
    for i in range(cells):
        value = at(result, i)
        pressure[i * planes : (i + 1) * planes, :] = value
        split(i, jnp.where(outside, value - at(measured, i).astype(F32), 0.0))
    copy_out = pltpu.make_async_copy(pressure, pressure_out, out_sems.at[0])
    copy_out.start()

    solve(1)

    def term(first):
        return viscosity[pl.ds(first, part), :].astype(F32) * result[pl.ds(first, part), :]

    for k in range(1, cases):
        other = (case + k) % cases
        value = term(pl.multiple_of(other * part, part))
        pack(rs_send.at[other], value[: part // 2], value[part // 2 :])
        send(rs_send.at[other], rs_got.at[case], 6, {"case": other})
    value = term(pl.multiple_of(case * part, part))
    pack(rs_got.at[case], value[: part // 2], value[part // 2 :])
    wait_bytes(rs_got.at[pl.ds(0, cases - 1)], recvs.at[6])
    upper, lower = unpack(rs_got.at[0])
    for k in range(1, cases):
        a, b = unpack(rs_got.at[k])
        upper, lower = upper + a, lower + b
    pack(ag_send, upper, lower)
    for k in range(1, cases):
        send(ag_send, ag_got.at[case], 7, {"case": (case + k) % cases})
    ag_got[case] = ag_send[...]
    for turn in range(2):
        wait_bytes(xs_got.at[turn, pl.ds(0, 2 * OUTER - 1)], sends.at[3 * turn])
        wait_bytes(hs_got.at[turn, pl.ds(0, MIDDLE - 1)], sends.at[3 * turn + 1])
        wait_bytes(cs_got.at[turn, 0], sends.at[3 * turn + 2])
    wait_bytes(rs_got.at[pl.ds(0, cases - 1)], sends.at[6])
    copy_out.wait()
    wait_bytes(ag_got.at[pl.ds(0, cases - 1)], recvs.at[7])
    for k in range(cases):
        a, b = unpack(ag_got.at[k])
        result[k * part : k * part + part // 2, :] = a
        result[k * part + part // 2 : (k + 1) * part, :] = b
    copy_out = pltpu.make_async_copy(result, gradient_out, out_sems.at[1])
    copy_out.start()
    wait_bytes(ag_got.at[pl.ds(0, cases - 1)], sends.at[7])
    copy_out.wait()


def shards(forcing, viscosity, measured, correction, wall_rows):
    cells, planes, rows = correction.shape
    spaces, cases = lax.axis_size("space"), lax.axis_size("case")
    assert spaces == 2 * OUTER * MIDDLE
    high, low = sine_tables(rows)
    modes = mode_table(rows, cells, cells * spaces, 1.0 / (2.0 * cells))
    flat = (cells * planes, rows)
    half, part = planes // 2, cells * planes // cases
    anywhere = pl.BlockSpec(memory_space=pl.ANY)
    pressure, gradient = pl.pallas_call(
        functools.partial(kernel, cases, cells, planes, rows),
        out_shape=(jax.ShapeDtypeStruct(flat, F32), jax.ShapeDtypeStruct(flat, F32)),
        in_specs=[anywhere] * 8,
        out_specs=(anywhere,) * 2,
        scratch_shapes=[
            pltpu.VMEM(flat, BF16),
            pltpu.VMEM(flat, BF16),
            pltpu.VMEM(flat, BF16),
            pltpu.VMEM(flat, F32),
            pltpu.VMEM((1, planes), I32),
            pltpu.VMEM((rows, rows), BF16),
            pltpu.VMEM((rows, rows), BF16),
            pltpu.VMEM(modes.shape, F32),
            pltpu.VMEM(flat, BF16),
            pltpu.VMEM(flat, BF16),
            pltpu.VMEM(flat, F32),
            pltpu.VMEM(flat, F32),
            pltpu.VMEM((2, 2, half, rows), F32),
            pltpu.VMEM(flat, F32),
            pltpu.VMEM((2, 2, half + 1, rows), I32),
            pltpu.VMEM((2, 2 * OUTER, half + 1, rows), I32),
            pltpu.VMEM((2, 2, half + 1, rows), I32),
            pltpu.VMEM((2, MIDDLE, half + 1, rows), I32),
            pltpu.VMEM((2, 2, half, rows), F32),
            pltpu.VMEM((2, 2, 2, half, rows), F32),
            pltpu.VMEM((cases, part // 2 + 1, rows), I32),
            pltpu.VMEM((cases, part // 2 + 1, rows), I32),
            pltpu.VMEM((part // 2 + 1, rows), I32),
            pltpu.VMEM((cases, part // 2 + 1, rows), I32),
            pltpu.SemaphoreType.DMA((8,)),
            pltpu.SemaphoreType.DMA((2,)),
            pltpu.SemaphoreType.DMA((8,)),
            pltpu.SemaphoreType.DMA((8,)),
        ],
        compiler_params=pltpu.CompilerParams(
            collective_id=0, has_side_effects=True, vmem_limit_bytes=60 * 1024 * 1024
        ),
    )(
        forcing.reshape(flat),
        viscosity.reshape(flat),
        measured.reshape(flat),
        correction.reshape(flat),
        wall_rows,
        jnp.asarray(high),
        jnp.asarray(low),
        jnp.asarray(modes),
    )
    return pressure.reshape(forcing.shape), gradient.reshape(correction.shape)


def solution(mesh):
    return jax.shard_map(
        shards,
        mesh=mesh,
        in_specs=(
            P("case", "space", None, None),
            P("case", "space", None, None),
            P("case", "space", None, None),
            P("space", None, None),
            P("case", None),
        ),
        out_specs=(P("case", "space", None, None), P("space", None, None)),
        check_vma=False,
    )
```

time: 78.1 us -> 64.1 us (0.82)
  Pallas kernels: 69.1 us -> 60.3 us
  local copies, waits for them, and re-layouts: 7.56 us -> 2.42 us
    pallas_call x1, Pallas kernels: 69.1 us -> 60.3 us  [shards(): pl.pallas_call(functools.partial(kernel, cases, cells, planes, rows), out...]
    unnamed x18 -> x4, local copies, waits for them, and re-layouts: 7.56 us -> 2.42 us
where the time goes in v2:
time: 64.1 us; the launch traced here: 63.4 us
  Pallas kernels  60.3 us (94%)
  local copies, waits for them, and re-layouts  2.42 us (4%)
  between operations  0.65 us (1%)
    pallas_call x1, Pallas kernels, shards(): pl.pallas_call(functools.partial(kernel, cases, cells, planes, rows), out...  60.3 us
    unnamed x4, local copies, waits for them, and re-layouts  2.42 us

profile of v2, /device:TPU:1, one launch (start us, length us, event | category | flops | bytes accessed | tf_op | source)
XLA Modules:
  0.0 63.4 jit_solution(15230736924634196253)
XLA Ops:
  0.6 60.3 %shard_map.95 = (f32[256,256]{1,0:T(8,128)}, f32[256,256]{1,0:T(8,128)}) custom-call(bf16[256,256]{1,0:T(8,128)(2,1)} %bitcast.9, bf16[256,256]{1,0:T(8,128)(2,1)} %bitcast.10, bf16[256,256]{1,0:T(8,128)(2,1)} %bitcast.11, f32[256,256]{1,0:T(8,128)} %bitcast.6, s32[1,32]{1,0:T(1,128)} %walls_in.1, bf16[256,256]{1,0:T(8,128)(2,1)} %constant.6.clone.high_in, ...), custom_call_target="tpu_custom_call" | custom-call | tf_op jit(solution)/shard_map/pallas_call | solution.py:278
  61.0 0.0 copy-start
  61.0 1.7 %copy.12 = f32[1,8,32,256]{3,2,1,0:T(8,128)} copy(f32[1,8,32,256]{3,2,1,0:T(8,128)} %bitcast.8) | data formatting | bytes 524288
  62.7 0.0 copy-done
  62.7 0.7 %copy.13 = f32[8,32,256]{2,1,0:T(8,128)} copy(f32[8,32,256]{2,1,0:T(8,128)S(1)} %bitcast.7) | data formatting | bytes 524288
Async XLA Ops:
  61.0 1.7 %copy-start = (f32[256,256]{1,0:T(8,128)S(1)}, f32[256,256]{1,0:T(8,128)}, u32[]{:S(2)}) copy-start(f32[256,256]{1,0:T(8,128)} %get-tuple-element.5) | copy-start | bytes 786436

commit v3 on v2

v3 whole, which is shorter than its diff:
```python
import functools

import jax
import jax.numpy as jnp
import ml_dtypes
import numpy as np
from jax import lax
from jax.experimental import pallas as pl
from jax.experimental.pallas import tpu as pltpu
from jax.sharding import PartitionSpec as P

MESH = pl.DeviceIdType.MESH
F32, BF16, I32 = jnp.float32, jnp.bfloat16, jnp.int32
OUTER, MIDDLE = 4, 4
TOP = 32767.0
LANES = 128
LIMIT = 16


def sine_tables(rows):
    index = np.arange(1, rows + 1, dtype=np.float64)
    phase = (index[:, None] * index[None, :]) % (2 * (rows + 1))
    sine = np.sqrt(2.0 / (rows + 1)) * np.sin(np.pi * phase / (rows + 1))
    high = sine.astype(ml_dtypes.bfloat16)
    low = (sine - high.astype(np.float64)).astype(ml_dtypes.bfloat16)
    return high, low


def mode_table(rows, cells, length, screen):
    index = np.arange(1, rows + 1, dtype=np.float64)
    centre = 4.0 * np.sin(np.pi * index / (2 * (rows + 1))) ** 2 + screen * screen
    rate = 1.0 + centre / 2.0 - np.sqrt(centre + centre * centre / 4.0)
    block = rate**cells
    lines = [
        rate,
        block,
        block**2,
        block ** (2 * MIDDLE),
        block ** (2 * MIDDLE * (OUTER - 1)),
        1.0 / (1.0 - rate**length),
        screen / (1.0 / rate - rate),
        np.zeros(rows),
    ]
    return np.stack(lines).astype(np.float32)


def wait_bytes(ref, sem):
    pltpu.make_async_copy(ref, ref, sem).wait()


def pack(first, second):
    largest = jnp.max(jnp.maximum(jnp.abs(first), jnp.abs(second)), axis=0, keepdims=True)
    code = jnp.ceil(jnp.log2(jnp.maximum(largest, 1e-30)) * 64.0)
    factor = TOP * jnp.exp2(code * (-1.0 / 64.0))
    a = jnp.round(first * factor).astype(I32)
    b = jnp.round(second * factor).astype(I32)
    return (a << 16) | (b & 0xFFFF), code.astype(I32)


def put(ref, first, second):
    words, code = pack(first, second)
    count, groups = words.shape[0], words.shape[1] // LANES
    for g in range(groups):
        ref[g * count : (g + 1) * count, :] = words[:, g * LANES : (g + 1) * LANES]
        ref[groups * count + g : groups * count + g + 1, :] = code[:, g * LANES : (g + 1) * LANES]


def take(ref, groups):
    count = ref.shape[0] // groups - 1
    first, second = [], []
    for g in range(groups):
        code = ref[groups * count + g : groups * count + g + 1, :]
        scale = jnp.exp2(code.astype(F32) * (1.0 / 64.0)) * (1.0 / TOP)
        words = ref[g * count : (g + 1) * count, :]
        first.append((words >> 16).astype(F32) * scale)
        second.append(((words << 16) >> 16).astype(F32) * scale)
    return jnp.concatenate(first, axis=1), jnp.concatenate(second, axis=1)


def kernel(cases, cells, planes, rows, forcing_in, viscosity_in, measured_in, correction_in, walls_in, high_in, low_in,
           modes_in, pressure_out, words_out, forcing, viscosity, measured, correction, walls, high_ref, low_ref, modes,
           head, tail, spectrum, result, moments, pressure, xs_send, xs_got, hs_send, hs_got, cs_send, cs_got,
           rs_send, rs_got, ag_send, in_sems, out_sems, sends, recvs):
    me = lax.axis_index("space")
    case = lax.axis_index("case")
    inner, middle, outer = me % 2, me // 2 % MIDDLE, me // (2 * MIDDLE)
    half = planes // 2
    groups = rows // LANES
    is_first = inner == 0

    def space(o, m, i):
        return {"space": (o * MIDDLE + m) * 2 + i}

    barrier = pltpu.get_barrier_semaphore()

    def greet(device):
        pl.semaphore_signal(barrier, inc=1, device_id=device, device_id_type=MESH)

    for k in (2, 1, 3):
        greet(space(outer, (middle + k) % MIDDLE, inner))
    loads = [
        pltpu.make_async_copy(src, dst, in_sems.at[i])
        for i, (src, dst) in enumerate(
            (
                (forcing_in, forcing),
                (viscosity_in, viscosity),
                (correction_in, correction),
                (high_in, high_ref),
                (low_in, low_ref),
                (modes_in, modes),
                (walls_in, walls),
                (measured_in, measured),
            )
        )
    ]
    for load in loads:
        load.start()
    for k in range(1, cases):
        greet({"case": (case + k) % cases})
    for k in range(1, 2 * OUTER):
        greet(space((outer + k // 2) % OUTER, middle, (inner + k) % 2))

    def lines(h, i):
        return pl.ds(pl.multiple_of(i * planes + h * half, half), half)

    def split(h, i, value):
        top = value.astype(BF16)
        head[h, i * half : (i + 1) * half, :] = top
        tail[h, i * half : (i + 1) * half, :] = (value - top.astype(F32)).astype(BF16)

    def sine(h):
        high, low = high_ref[...], low_ref[...]
        top = head[h]
        small = jnp.dot(top, low, preferred_element_type=F32) + jnp.dot(tail[h], high, preferred_element_type=F32)
        return jnp.dot(top, high, preferred_element_type=F32) + small

    def at(ref, h, i):
        return ref[h, i * half : (i + 1) * half, :]

    def line(i):
        return modes[i : i + 1, :]

    def send(src, dst, phase, device):
        pltpu.make_async_remote_copy(
            src_ref=src, dst_ref=dst, send_sem=sends.at[phase], recv_sem=recvs.at[phase], device_id=device, device_id_type=MESH
        ).start()

    def begin(turn, h):
        spectrum[h] = sine(h)
        rate = line(0)
        onward = rate * at(spectrum, h, 0)
        backward = rate * at(spectrum, h, cells - 1)
        for i in range(1, cells):
            onward = (onward + at(spectrum, h, i)) * rate
            backward = (backward + at(spectrum, h, cells - 1 - i)) * rate
        moments[0, h] = onward
        moments[1, h] = backward
        put(xs_send.at[turn, h], onward, backward)

    def send_moments(turn, h, steps):
        for d in steps:
            send(
                xs_send.at[turn, h], xs_got.at[turn, 2 * outer + inner], 3 * turn, space((outer + d) % OUTER, middle, h)
            )

    def cross(turn):
        first = 3 * turn
        wait_bytes(xs_got.at[turn, pl.ds(0, 2 * OUTER - 1)], recvs.at[first])
        block, two, eight, most = line(1), line(2), line(3), line(4)
        own_l, own_r = moments[0, inner], moments[1, inner]
        other_l, other_r = take(xs_got.at[turn, 2 * outer + 1 - inner], groups)
        l0, l1 = jnp.where(is_first, own_l, other_l), jnp.where(is_first, other_l, own_l)
        r0, r1 = jnp.where(is_first, own_r, other_r), jnp.where(is_first, other_r, own_r)
        chip_l, chip_r = l0 * block + l1, r0 + r1 * block
        pairs = []
        for d in range(1, OUTER):
            slot = 2 * ((outer + d) % OUTER)
            a_l, a_r = take(xs_got.at[turn, slot], groups)
            b_l, b_r = take(xs_got.at[turn, slot + 1], groups)
            pairs.append((a_l * block + b_l, a_r + b_r * block))
        before = pairs[0][0]
        after = pairs[OUTER - 2][1]
        for d in range(1, OUTER - 1):
            before = pairs[d][0] + eight * before
            after = pairs[OUTER - 2 - d][1] + eight * after
        onto, round_l = chip_l + eight * before, before + most * chip_l
        back, round_r = chip_r + eight * after, after + most * chip_r
        put(hs_send.at[turn, 0], onto, round_r)
        put(hs_send.at[turn, 1], round_l, back)
        for k in (2, 1, 3):
            send(
                hs_send.at[turn, (middle + k) // MIDDLE],
                hs_got.at[turn, middle],
                first + 1,
                space(outer, (middle + k) % MIDDLE, inner),
            )
        wait_bytes(hs_got.at[turn, pl.ds(0, MIDDLE - 1)], recvs.at[first + 1])
        near = [take(hs_got.at[turn, (middle + d) % MIDDLE], groups) for d in range(1, MIDDLE)]
        left, right = round_l, round_r
        for d in range(1, MIDDLE):
            left = near[d - 1][0] + two * left
            right = near[MIDDLE - 1 - d][1] + two * right
        left, right = left * line(5), right * line(5)
        left_1, right_0 = left * block + l0, right * block + r1
        cs_send[turn, 0] = jnp.where(is_first, left_1, left)
        cs_send[turn, 1] = jnp.where(is_first, right, right_0)
        send(cs_send.at[turn], cs_got.at[turn], first + 2, space(outer, middle, 1 - inner))
        return jnp.where(is_first, left, left_1), jnp.where(is_first, right_0, right)

    def finish(h, left, right):
        rate = line(0)
        running = right
        for i in range(cells - 1, -1, -1):
            result[h, i * half : (i + 1) * half, :] = running
            running = (running + at(spectrum, h, i)) * rate
        running = left
        for i in range(cells):
            running = at(spectrum, h, i) + (running if i == 0 else running * rate)
            split(h, i, (running + at(result, h, i)) * line(6))
        result[h] = sine(h)

    def misfit(h):
        chosen = lax.broadcasted_iota(I32, (half, planes), 0) + h * half == lax.broadcasted_iota(I32, (half, planes), 1)
        first_row = jnp.sum(jnp.where(chosen, walls[...], 0), axis=1, keepdims=True)
        outside = lax.broadcasted_iota(I32, (half, rows), 1) >= first_row
        for i in range(cells):
            value = at(result, h, i)
            pressure[lines(h, i), :] = value
            split(h, i, jnp.where(outside, value - measured[lines(h, i), :].astype(F32), 0.0))

    def give(h):
        for i in range(cells):
            value = viscosity[lines(h, i), :].astype(F32) * at(result, h, i)
            put(rs_send.at[h * cells + i], value[: half // 2], value[half // 2 :])
        for k in range(cells):
            other = h * cells + (case + k) % cells

            @pl.when(other != case)
            def _():
                send(rs_send.at[other], rs_got.at[case], 6, {"case": other})

    for i in range(3):
        loads[i].wait()
    for i in range(cells):
        for h in range(2):
            rows_in = lines(h, i)
            split(h, i, forcing[rows_in, :].astype(F32) + viscosity[rows_in, :].astype(F32) * correction[rows_in, :])
    for i in range(3, 8):
        loads[i].wait()
    for h in range(2):
        begin(0, h)
    pl.semaphore_wait(barrier, cases - 1 + MIDDLE - 1 + 2 * OUTER - 1)
    send_moments(0, inner, (2, 1, 3))
    send_moments(0, 1 - inner, (2, 1, 3, 0))
    left, right = cross(0)
    finish(inner, left, right)
    misfit(inner)
    begin(1, inner)
    send_moments(1, inner, (2, 1, 3))
    wait_bytes(cs_got.at[0], recvs.at[2])
    finish(1 - inner, cs_got[0, 0], cs_got[0, 1])
    misfit(1 - inner)
    begin(1, 1 - inner)
    send_moments(1, 1 - inner, (2, 1, 3, 0))
    copy_out = pltpu.make_async_copy(pressure, pressure_out, out_sems.at[0])
    copy_out.start()
    left, right = cross(1)
    finish(inner, left, right)
    give(inner)
    wait_bytes(cs_got.at[1], recvs.at[5])
    finish(1 - inner, cs_got[1, 0], cs_got[1, 1])
    give(1 - inner)
    rs_got[case] = rs_send[case]
    for turn in range(2):
        wait_bytes(xs_got.at[turn, pl.ds(0, 2 * OUTER - 1)], sends.at[3 * turn])
        wait_bytes(hs_got.at[turn, pl.ds(0, MIDDLE - 1)], sends.at[3 * turn + 1])
        wait_bytes(cs_got.at[turn], sends.at[3 * turn + 2])
    copy_out.wait()
    wait_bytes(rs_got.at[pl.ds(0, cases - 1)], recvs.at[6])
    upper, lower = take(rs_got.at[0], groups)
    for k in range(1, cases):
        a, b = take(rs_got.at[k], groups)
        upper, lower = upper + a, lower + b
    put(ag_send, upper, lower)
    for k in range(1, cases):
        send(ag_send, words_out.at[case], 7, {"case": (case + k) % cases})
    keep = pltpu.make_async_copy(ag_send, words_out.at[case], out_sems.at[1])
    keep.start()
    wait_bytes(rs_got.at[pl.ds(0, cases - 1)], sends.at[6])
    keep.wait()
    wait_bytes(words_out.at[pl.ds(0, cases - 1)], recvs.at[7])
    wait_bytes(words_out.at[pl.ds(0, cases - 1)], sends.at[7])


def spread(cells, planes, pressure_in, words, pressure_out, gradient_out, gradient, sems):
    copies = [pltpu.make_async_copy(pressure_in, pressure_out, sems.at[0])]
    copies[0].start()
    half = planes // 2
    for h in range(2):
        for i in range(cells):
            a, b = take(words.at[h * cells + i], gradient.shape[1] // LANES)
            start = i * planes + h * half
            gradient[start : start + half // 2, :] = a
            gradient[start + half // 2 : start + half, :] = b
    copies.append(pltpu.make_async_copy(gradient, gradient_out, sems.at[1]))
    copies[1].start()
    for copy in copies:
        copy.wait()


def shards(forcing, viscosity, measured, correction, wall_rows):
    cells, planes, rows = correction.shape
    spaces, cases = lax.axis_size("space"), lax.axis_size("case")
    assert spaces == 2 * OUTER * MIDDLE and cases == 2 * cells
    high, low = sine_tables(rows)
    modes = mode_table(rows, cells, cells * spaces, 1.0 / (2.0 * cells))
    flat = (cells * planes, rows)
    half, groups = planes // 2, rows // LANES
    halves = (2, cells * half, rows)
    message = (groups * (half + 1), LANES)
    short = (groups * (half // 2 + 1), LANES)
    there = pl.BlockSpec(memory_space=pltpu.HBM)
    anywhere = pl.BlockSpec(memory_space=pl.ANY)
    pressure, words = pl.pallas_call(
        functools.partial(kernel, cases, cells, planes, rows),
        out_shape=(jax.ShapeDtypeStruct(flat, F32), jax.ShapeDtypeStruct((cases, *short), I32)),
        in_specs=[there] * 8,
        out_specs=(anywhere,) * 2,
        scratch_shapes=[
            pltpu.VMEM(flat, BF16),
            pltpu.VMEM(flat, BF16),
            pltpu.VMEM(flat, BF16),
            pltpu.VMEM(flat, F32),
            pltpu.VMEM((1, planes), I32),
            pltpu.VMEM((rows, rows), BF16),
            pltpu.VMEM((rows, rows), BF16),
            pltpu.VMEM(modes.shape, F32),
            pltpu.VMEM(halves, BF16),
            pltpu.VMEM(halves, BF16),
            pltpu.VMEM(halves, F32),
            pltpu.VMEM(halves, F32),
            pltpu.VMEM((2, 2, half, rows), F32),
            pltpu.VMEM(flat, F32),
            pltpu.VMEM((2, 2, *message), I32),
            pltpu.VMEM((2, 2 * OUTER, *message), I32),
            pltpu.VMEM((2, 2, *message), I32),
            pltpu.VMEM((2, MIDDLE, *message), I32),
            pltpu.VMEM((2, 2, half, rows), F32),
            pltpu.VMEM((2, 2, half, rows), F32),
            pltpu.VMEM((cases, *short), I32),
            pltpu.VMEM((cases, *short), I32),
            pltpu.VMEM(short, I32),
            pltpu.SemaphoreType.DMA((8,)),
            pltpu.SemaphoreType.DMA((2,)),
            pltpu.SemaphoreType.DMA((8,)),
            pltpu.SemaphoreType.DMA((8,)),
        ],
        compiler_params=pltpu.CompilerParams(
            collective_id=0, has_side_effects=True, vmem_limit_bytes=LIMIT * 1024 * 1024
        ),
    )(
        *(pltpu.with_memory_space_constraint(x, pltpu.HBM) for x in (forcing.reshape(flat),
        viscosity.reshape(flat),
        measured.reshape(flat),
        correction.reshape(flat),
        wall_rows,
        jnp.asarray(high),
        jnp.asarray(low),
        jnp.asarray(modes))),
    )
    pressure, gradient = pl.pallas_call(
        functools.partial(spread, cells, planes),
        out_shape=(jax.ShapeDtypeStruct(flat, F32), jax.ShapeDtypeStruct(flat, F32)),
        in_specs=[anywhere, pl.BlockSpec(memory_space=pltpu.VMEM)],
        out_specs=(anywhere,) * 2,
        scratch_shapes=[pltpu.VMEM(flat, F32), pltpu.SemaphoreType.DMA((2,))],
        compiler_params=pltpu.CompilerParams(vmem_limit_bytes=LIMIT * 1024 * 1024),
    )(pressure, words)
    return pressure.reshape(forcing.shape), gradient.reshape(correction.shape)


def solution(mesh):
    return jax.shard_map(
        shards,
        mesh=mesh,
        in_specs=(
            P("case", "space", None, None),
            P("case", "space", None, None),
            P("case", "space", None, None),
            P("space", None, None),
            P("case", None),
        ),
        out_specs=(P("case", "space", None, None), P("space", None, None)),
        check_vma=False,
    )
```

time: 64.1 us -> 55.3 us (0.86)
  Pallas kernels: 60.3 us -> 54.5 us
  local copies, waits for them, and re-layouts: 2.42 us -> 0 us
    pallas_call x1, Pallas kernels: 60.3 us -> 53.7 us  [shards(): pl.pallas_call(functools.partial(kernel, cases, cells, planes, rows), out...]
    unnamed x4 -> x0, local copies, waits for them, and re-layouts: 2.42 us -> none
    pallas_call x0 -> x1, Pallas kernels: none -> 0.81 us  [shards(): pl.pallas_call(functools.partial(spread, cells, planes), out_shape=(jax.S...]
where the time goes in v3:
time: 55.3 us; the launch traced here: 55.1 us
  Pallas kernels  54.5 us (99%)
  between operations  0.64 us (1%)
    pallas_call x1, Pallas kernels, shards(): pl.pallas_call(functools.partial(kernel, cases, cells, planes, rows), out...  53.7 us

profile of v3, /device:TPU:1, one launch (start us, length us, event | category | flops | bytes accessed | tf_op | source)
XLA Modules:
  0.0 55.1 jit_solution(2139872745486736652)
XLA Ops:
  0.6 53.7 %shard_map.95 = (f32[256,256]{1,0:T(8,128)S(1)}, s32[16,18,128]{2,1,0:T(8,128)S(1)}) custom-call(bf16[256,256]{1,0:T(8,128)(2,1)} %bitcast.7, bf16[256,256]{1,0:T(8,128)(2,1)} %bitcast.8, bf16[256,256]{1,0:T(8,128)(2,1)} %bitcast.9, f32[256,256]{1,0:T(8,128)} %bitcast.6, s32[1,32]{1,0:T(1,128)} %walls_in.1, bf16[256,256]{1,0:T(8,128)(2,1)} %constant.6.clone.high_in, ...), custom_call_target="tpu_custom_call" | custom-call | tf_op jit(solution)/shard_map/pallas_call | solution.py:324
  54.3 0.8 %shard_map.96 = (f32[256,256]{1,0:T(8,128)}, f32[256,256]{1,0:T(8,128)}) custom-call(f32[256,256]{1,0:T(8,128)S(1)} %get-tuple-element.6.pressure_in, s32[16,18,128]{2,1,0:T(8,128)S(1)} %get-tuple-element.7.words), custom_call_target="tpu_custom_call" | custom-call | tf_op jit(solution)/shard_map/pallas_call | solution.py:371

commit v4 on v3

v4 whole, which is shorter than its diff:
```python
import functools

import jax
import jax.numpy as jnp
import ml_dtypes
import numpy as np
from jax import lax
from jax.experimental import pallas as pl
from jax.experimental.pallas import tpu as pltpu
from jax.sharding import PartitionSpec as P

MESH = pl.DeviceIdType.MESH
F32, BF16, I32 = jnp.float32, jnp.bfloat16, jnp.int32
OUTER, MIDDLE = 4, 4
TOP = 32767.0
LANES = 128
LIMIT = 16


def sine_tables(rows):
    index = np.arange(1, rows + 1, dtype=np.float64)
    phase = (index[:, None] * index[None, :]) % (2 * (rows + 1))
    sine = np.sqrt(2.0 / (rows + 1)) * np.sin(np.pi * phase / (rows + 1))
    high = sine.astype(ml_dtypes.bfloat16)
    low = (sine - high.astype(np.float64)).astype(ml_dtypes.bfloat16)
    return high, low


def mode_table(rows, cells, length, screen):
    index = np.arange(1, rows + 1, dtype=np.float64)
    centre = 4.0 * np.sin(np.pi * index / (2 * (rows + 1))) ** 2 + screen * screen
    rate = 1.0 + centre / 2.0 - np.sqrt(centre + centre * centre / 4.0)
    lines = [rate, 1.0 / (1.0 - rate**length), screen / (1.0 / rate - rate)]
    step = 1
    while step < length // cells:
        lines.append(rate ** (cells * step))
        step *= 2
    table = np.zeros((-(-len(lines) // 8) * 8, rows))
    table[: len(lines)] = lines
    return table.astype(np.float32)


def wait_bytes(ref, sem):
    pltpu.make_async_copy(ref, ref, sem).wait()


def pack(first, second):
    largest = jnp.max(jnp.maximum(jnp.abs(first), jnp.abs(second)), axis=0, keepdims=True)
    code = jnp.ceil(jnp.log2(jnp.maximum(largest, 1e-30)) * 64.0)
    factor = TOP * jnp.exp2(code * (-1.0 / 64.0))
    a = jnp.round(first * factor).astype(I32)
    b = jnp.round(second * factor).astype(I32)
    return (a << 16) | (b & 0xFFFF), code.astype(I32)


def put(ref, first, second):
    words, code = pack(first, second)
    count, groups = words.shape[0], words.shape[1] // LANES
    for g in range(groups):
        ref[g * count : (g + 1) * count, :] = words[:, g * LANES : (g + 1) * LANES]
        ref[groups * count + g : groups * count + g + 1, :] = code[:, g * LANES : (g + 1) * LANES]


def take(ref, groups):
    count = ref.shape[0] // groups - 1
    first, second = [], []
    for g in range(groups):
        code = ref[groups * count + g : groups * count + g + 1, :]
        scale = jnp.exp2(code.astype(F32) * (1.0 / 64.0)) * (1.0 / TOP)
        words = ref[g * count : (g + 1) * count, :]
        first.append((words >> 16).astype(F32) * scale)
        second.append(((words << 16) >> 16).astype(F32) * scale)
    return jnp.concatenate(first, axis=1), jnp.concatenate(second, axis=1)


def kernel(cases, cells, planes, rows, forcing_in, viscosity_in, measured_in, correction_in, walls_in, high_in, low_in,
           modes_in, pressure_out, words_out, forcing, viscosity, measured, correction, walls, high_ref, low_ref, modes,
           head, tail, spectrum, result, pressure, walls_send, walls_got, a_send, a_got, b_send, b_got,
           rs_send, rs_got, ag_send, in_sems, out_sems, sends, recvs):
    me = lax.axis_index("space")
    case = lax.axis_index("case")
    inner, middle, outer = me % 2, me // 2 % MIDDLE, me // (2 * MIDDLE)
    half = planes // 2
    groups = rows // LANES
    spaces = 2 * OUTER * MIDDLE
    partner = (case + cases // 2) % cases
    upper_case = case // (cases // 2)
    owned = (outer * MIDDLE + (middle + MIDDLE - 1 + upper_case) % MIDDLE) * 2 + inner

    def solver(plane):
        o, m, i = plane // (2 * MIDDLE), plane // 2 % MIDDLE, plane % 2
        return {"case": partner, "space": (o * MIDDLE + (m + upper_case) % MIDDLE) * 2 + i}

    def nearby(steps):
        return [(o, m, i) for m in steps for o in (2, 1, 3, 0) for i in (1, 0)]

    barrier = pltpu.get_barrier_semaphore()

    def greet(device):
        pl.semaphore_signal(barrier, inc=1, device_id=device, device_id_type=MESH)

    def place(o, m, i):
        return (((outer + o) % OUTER) * MIDDLE + (middle + m) % MIDDLE) * 2 + (inner + i) % 2

    loads = [
        pltpu.make_async_copy(src, dst, in_sems.at[i])
        for i, (src, dst) in enumerate(
            (
                (forcing_in, forcing),
                (viscosity_in, viscosity),
                (correction_in, correction),
                (high_in, high_ref),
                (low_in, low_ref),
                (modes_in, modes),
                (walls_in, walls),
                (measured_in, measured),
            )
        )
    ]
    for load in loads[:3]:
        load.start()
    for o, m, i in nearby((1, 2, 3, 0)):
        greet({"case": partner, "space": place(o, m + upper_case, i)})
    for load in loads[3:]:
        load.start()
    for k in range(1, cases):
        greet({"case": (case + k) % cases})

    def lines(h, i):
        start = i * planes + h * half
        return slice(start, start + half)

    def split(h, i, value):
        count = value.shape[0]
        top = value.astype(BF16)
        head[h, i * count : (i + 1) * count, :] = top
        tail[h, i * count : (i + 1) * count, :] = (value - top.astype(F32)).astype(BF16)

    def sine(h):
        high, low = high_ref[...], low_ref[...]
        top = head[h]
        small = jnp.dot(top, low, preferred_element_type=F32) + jnp.dot(tail[h], high, preferred_element_type=F32)
        return jnp.dot(top, high, preferred_element_type=F32) + small

    def at(ref, h, i):
        return ref[h, i * half : (i + 1) * half, :]

    def line(i):
        return modes[i : i + 1, :]

    def send(src, dst, phase, device):
        pltpu.make_async_remote_copy(
            src_ref=src, dst_ref=dst, send_sem=sends.at[phase], recv_sem=recvs.at[phase], device_id=device, device_id_type=MESH
        ).start()

    def lay(ref, where, k, value):
        for g in range(groups):
            ref[where, k * groups + g, :] = value[:, g * LANES : (g + 1) * LANES]

    def lift(ref, where, k):
        return jnp.concatenate([ref[where, k * groups + g, :] for g in range(groups)], axis=1)

    def block_moments(ref, h):
        rate = line(0)
        onward = rate * at(ref, h, 0)
        backward = rate * at(ref, h, cells - 1)
        for i in range(1, cells):
            onward = (onward + at(ref, h, i)) * rate
            backward = (backward + at(ref, h, cells - 1 - i)) * rate
        return onward, backward

    def finish(ref, h, left=None, right=None):
        rate = line(0)
        running = right
        for i in range(cells - 1, -1, -1):
            if running is not None:
                result[h, i * half : (i + 1) * half, :] = running
            running = (at(ref, h, i) if running is None else running + at(ref, h, i)) * rate
        running = left
        for i in range(cells):
            value = at(ref, h, i)
            running = value if running is None else value + (running if i == 0 else running * rate)
            full = running if right is None and i == cells - 1 else running + at(result, h, i)
            split(h, i, full * line(2))
        result[h] = sine(h)

    def misfit(h, keep):
        chosen = lax.broadcasted_iota(I32, (half, planes), 0) + h * half == lax.broadcasted_iota(I32, (half, planes), 1)
        first_row = jnp.sum(jnp.where(chosen, walls[...], 0), axis=1, keepdims=True)
        outside = lax.broadcasted_iota(I32, (half, rows), 1) >= first_row
        for i in range(cells):
            value = at(result, h, i)
            if keep:
                pressure[lines(h, i), :] = value
            split(h, i, jnp.where(outside, value - measured[lines(h, i), :].astype(F32), 0.0))

    def give(h):
        for i in range(cells):
            value = viscosity[lines(h, i), :].astype(F32) * at(result, h, i)
            put(rs_send.at[h * cells + i], value[: half // 2], value[half // 2 :])
        for k in range(cells):
            other = h * cells + (case + k) % cells

            @pl.when(other != case)
            def _():
                send(rs_send.at[other], rs_got.at[case], 2, {"case": other})

    for i in range(3):
        loads[i].wait()
    for h in range(2):
        for i in range(cells):
            part = lines(h, i)
            split(h, i, forcing[part, :].astype(F32) + viscosity[part, :].astype(F32) * correction[part, :])
    for i in range(3, 8):
        loads[i].wait()
    walls_send[...] = jnp.zeros_like(walls_send)
    walls_send[:, 0:planes] = walls[...]
    for h in range(2):
        some = slice(h * half, (h + 1) * half)
        spectrum[h] = sine(h)
        onward, backward = block_moments(spectrum, h)
        lay(a_send, some, 0, onward)
        lay(a_send, some, 1, backward)
        finish(spectrum, h)
        misfit(h, False)
        result[h] = sine(h)
        onward, backward = block_moments(result, h)
        lay(a_send, some, 2, onward)
        lay(a_send, some, 3, backward)
    pl.semaphore_wait(barrier, cases - 1 + spaces)
    send(walls_send, walls_got, 4, solver(me))
    for o, m, i in nearby((1, 2, 3, 0)):
        plane = place(o, m, i)
        send(a_send.at[plane], a_got.at[me], 0, solver(plane))

    wait_bytes(walls_got, recvs.at[4])
    chosen = lax.broadcasted_iota(I32, walls_got.shape, 1) == owned
    first_row = jnp.sum(jnp.where(chosen, walls_got[...], 0), axis=1, keepdims=True)
    outside = lax.broadcasted_iota(I32, (1, rows), 1) >= first_row
    wait_bytes(a_got, recvs.at[0])
    every = slice(0, spaces)

    def scan(onward, backward):
        step, k = 1, 3
        while step < spaces:
            onward = onward + line(k) * pltpu.roll(onward, step, 0)
            backward = backward + line(k) * pltpu.roll(backward, spaces - step, 0)
            step, k = 2 * step, k + 1
        return pltpu.roll(onward, 1, 0) * line(1), pltpu.roll(backward, spaces - 1, 0) * line(1)

    rate = line(0)
    left, right = scan(lift(a_got, every, 0), lift(a_got, every, 1))
    lay(b_send, every, 0, left)
    lay(b_send, every, 1, right)
    quarter = cells // 2
    powers = [line(2)]
    for i in range(1, cells):
        powers.append(powers[-1] * rate)
    for i in range(cells):
        split(i // quarter, i % quarter, left * powers[i] + right * powers[cells - 1 - i])

    def row_block(i):
        return result[i // quarter, (i % quarter) * spaces : (i % quarter + 1) * spaces, :]

    for h in range(2):
        result[h] = sine(h)
    for i in range(cells):
        split(i // quarter, i % quarter, jnp.where(outside, row_block(i), 0.0))
    for h in range(2):
        result[h] = sine(h)
    onward, backward = rate * row_block(0), rate * row_block(cells - 1)
    for i in range(1, cells):
        onward = (onward + row_block(i)) * rate
        backward = (backward + row_block(cells - 1 - i)) * rate
    left, right = scan(lift(a_got, every, 2) + onward, lift(a_got, every, 3) + backward)
    lay(b_send, every, 2, left)
    lay(b_send, every, 3, right)
    for o, m, i in nearby((1, 2, 3, 0)):
        target = place(o, m + upper_case, i)
        send(b_send.at[target], b_got.at[owned], 1, {"case": partner, "space": target})
    wait_bytes(b_got, recvs.at[1])

    for h in range(2):
        some = slice(h * half, (h + 1) * half)
        finish(spectrum, h, lift(b_got, some, 0), lift(b_got, some, 1))
        misfit(h, True)
        spectrum[h] = sine(h)
        finish(spectrum, h, lift(b_got, some, 2), lift(b_got, some, 3))
        give(h)
    copy_out = pltpu.make_async_copy(pressure, pressure_out, out_sems.at[0])
    copy_out.start()
    rs_got[case] = rs_send[case]
    wait_bytes(a_got, sends.at[0])
    wait_bytes(b_got, sends.at[1])
    wait_bytes(walls_got, sends.at[4])
    wait_bytes(rs_got.at[pl.ds(0, cases - 1)], recvs.at[2])
    upper, lower = take(rs_got.at[0], groups)
    for k in range(1, cases):
        a, b = take(rs_got.at[k], groups)
        upper, lower = upper + a, lower + b
    put(ag_send, upper, lower)
    for k in range(1, cases):
        send(ag_send, words_out.at[case], 3, {"case": (case + k) % cases})
    keep = pltpu.make_async_copy(ag_send, words_out.at[case], out_sems.at[1])
    keep.start()
    wait_bytes(rs_got.at[pl.ds(0, cases - 1)], sends.at[2])
    copy_out.wait()
    keep.wait()
    wait_bytes(words_out.at[pl.ds(0, cases - 1)], recvs.at[3])
    wait_bytes(words_out.at[pl.ds(0, cases - 1)], sends.at[3])


def spread(cells, planes, pressure_in, words, pressure_out, gradient_out, gradient, sems):
    copies = [pltpu.make_async_copy(pressure_in, pressure_out, sems.at[0])]
    copies[0].start()
    half = planes // 2
    for h in range(2):
        for i in range(cells):
            a, b = take(words.at[h * cells + i], gradient.shape[1] // LANES)
            start = i * planes + h * half
            gradient[start : start + half // 2, :] = a
            gradient[start + half // 2 : start + half, :] = b
    copies.append(pltpu.make_async_copy(gradient, gradient_out, sems.at[1]))
    copies[1].start()
    for copy in copies:
        copy.wait()


def shards(forcing, viscosity, measured, correction, wall_rows):
    cells, planes, rows = correction.shape
    spaces, cases = lax.axis_size("space"), lax.axis_size("case")
    assert spaces == 2 * OUTER * MIDDLE and cases == 2 * cells
    high, low = sine_tables(rows)
    modes = mode_table(rows, cells, cells * spaces, 1.0 / (2.0 * cells))
    flat = (cells * planes, rows)
    half, groups = planes // 2, rows // LANES
    halves = (2, cells * half, rows)
    short = (groups * (half // 2 + 1), LANES)
    there = pl.BlockSpec(memory_space=pltpu.HBM)
    anywhere = pl.BlockSpec(memory_space=pl.ANY)
    pressure, words = pl.pallas_call(
        functools.partial(kernel, cases, cells, planes, rows),
        out_shape=(jax.ShapeDtypeStruct(flat, F32), jax.ShapeDtypeStruct((cases, *short), I32)),
        in_specs=[there] * 8,
        out_specs=(anywhere,) * 2,
        scratch_shapes=[
            pltpu.VMEM(flat, BF16),
            pltpu.VMEM(flat, BF16),
            pltpu.VMEM(flat, BF16),
            pltpu.VMEM(flat, F32),
            pltpu.VMEM((1, planes), I32),
            pltpu.VMEM((rows, rows), BF16),
            pltpu.VMEM((rows, rows), BF16),
            pltpu.VMEM(modes.shape, F32),
            pltpu.VMEM(halves, BF16),
            pltpu.VMEM(halves, BF16),
            pltpu.VMEM(halves, F32),
            pltpu.VMEM(halves, F32),
            pltpu.VMEM(flat, F32),
            pltpu.VMEM((1, LANES), I32),
            pltpu.VMEM((1, LANES), I32),
            *[pltpu.VMEM((spaces, 4 * groups, LANES), F32)] * 4,
            pltpu.VMEM((cases, *short), I32),
            pltpu.VMEM((cases, *short), I32),
            pltpu.VMEM(short, I32),
            pltpu.SemaphoreType.DMA((8,)),
            pltpu.SemaphoreType.DMA((2,)),
            pltpu.SemaphoreType.DMA((5,)),
            pltpu.SemaphoreType.DMA((5,)),
        ],
        compiler_params=pltpu.CompilerParams(
            collective_id=0, has_side_effects=True, vmem_limit_bytes=LIMIT * 1024 * 1024
        ),
    )(
        *(pltpu.with_memory_space_constraint(x, pltpu.HBM) for x in (forcing.reshape(flat),
        viscosity.reshape(flat),
        measured.reshape(flat),
        correction.reshape(flat),
        wall_rows,
        jnp.asarray(high),
        jnp.asarray(low),
        jnp.asarray(modes))),
    )
    pressure, gradient = pl.pallas_call(
        functools.partial(spread, cells, planes),
        out_shape=(jax.ShapeDtypeStruct(flat, F32), jax.ShapeDtypeStruct(flat, F32)),
        in_specs=[anywhere, pl.BlockSpec(memory_space=pltpu.VMEM)],
        out_specs=(anywhere,) * 2,
        scratch_shapes=[pltpu.VMEM(flat, F32), pltpu.SemaphoreType.DMA((2,))],
        compiler_params=pltpu.CompilerParams(vmem_limit_bytes=LIMIT * 1024 * 1024),
    )(pressure, words)
    return pressure.reshape(forcing.shape), gradient.reshape(correction.shape)


def solution(mesh):
    return jax.shard_map(
        shards,
        mesh=mesh,
        in_specs=(
            P("case", "space", None, None),
            P("case", "space", None, None),
            P("case", "space", None, None),
            P("space", None, None),
            P("case", None),
        ),
        out_specs=(P("case", "space", None, None), P("space", None, None)),
        check_vma=False,
    )
```

time: 55.3 us -> 51.1 us (0.924)
  Pallas kernels: 54.5 us -> 50.3 us
    pallas_call x1, Pallas kernels: 53.7 us -> 49.5 us  [shards(): pl.pallas_call(functools.partial(kernel, cases, cells, planes, rows), out...]
where the time goes in v4:
time: 51.1 us; the launch traced here: 51 us
  Pallas kernels  50.3 us (98%)
  between operations  0.64 us (1%)
    pallas_call x1, Pallas kernels, shards(): pl.pallas_call(functools.partial(kernel, cases, cells, planes, rows), out...  49.5 us

profile of v4, /device:TPU:1, one launch (start us, length us, event | category | flops | bytes accessed | tf_op | source)
XLA Modules:
  0.0 51.0 jit_solution(9778293333348149892)
XLA Ops:
  0.6 49.5 %shard_map.95 = (f32[256,256]{1,0:T(8,128)S(1)}, s32[16,18,128]{2,1,0:T(8,128)S(1)}) custom-call(bf16[256,256]{1,0:T(8,128)(2,1)} %bitcast.7, bf16[256,256]{1,0:T(8,128)(2,1)} %bitcast.8, bf16[256,256]{1,0:T(8,128)(2,1)} %bitcast.9, f32[256,256]{1,0:T(8,128)} %bitcast.6, s32[1,32]{1,0:T(1,128)} %walls_in.1, bf16[256,256]{1,0:T(8,128)(2,1)} %constant.6.clone.high_in, ...), custom_call_target="tpu_custom_call" | custom-call | tf_op jit(solution)/shard_map/pallas_call | solution.py:341
  50.2 0.8 %shard_map.96 = (f32[256,256]{1,0:T(8,128)}, f32[256,256]{1,0:T(8,128)}) custom-call(f32[256,256]{1,0:T(8,128)S(1)} %get-tuple-element.6.pressure_in, s32[16,18,128]{2,1,0:T(8,128)S(1)} %get-tuple-element.7.words), custom_call_target="tpu_custom_call" | custom-call | tf_op jit(solution)/shard_map/pallas_call | solution.py:384

commit v5 on v4

--- a/solution.py
+++ b/solution.py
@@ -14,6 +14,7 @@
 OUTER, MIDDLE = 4, 4
 TOP = 32767.0
 LANES = 128
+SEGMENT = 16
 LIMIT = 16
 
 
@@ -127,8 +128,11 @@
         greet({"case": (case + k) % cases})
 
     def lines(h, i):
-        start = i * planes + h * half
-        return slice(start, start + half)
+        return pl.ds(pl.multiple_of(i * planes + h * half, half), half)
+
+    def case_at(far, step, y):
+        bit = (case // 4 + step) % 2
+        return (upper_case + far) % 2 * (cases // 2) + bit * 4 + (case + y) % 4
 
     def split(h, i, value):
         count = value.shape[0]
@@ -153,12 +157,46 @@
             src_ref=src, dst_ref=dst, send_sem=sends.at[phase], recv_sem=recvs.at[phase], device_id=device, device_id_type=MESH
         ).start()
 
-    def lay(ref, where, k, value):
-        for g in range(groups):
-            ref[where, k * groups + g, :] = value[:, g * LANES : (g + 1) * LANES]
-
-    def lift(ref, where, k):
-        return jnp.concatenate([ref[where, k * groups + g, :] for g in range(groups)], axis=1)
+    def segments(axis):
+        return lax.broadcasted_iota(I32, (LANES, LANES), axis) // SEGMENT
+
+    segment_sum = (segments(0) == segments(1)).astype(BF16)
+
+    def lay(ref, where, *pairs):
+        codes = None
+        for p, pair in enumerate(pairs):
+            for g in range(groups):
+                first, second = (value[:, g * LANES : (g + 1) * LANES] for value in pair)
+                square = jnp.dot(
+                    (first * first + second * second).astype(BF16), segment_sum, preferred_element_type=F32
+                )
+                code = jnp.ceil(2.0 * jnp.log2(jnp.maximum(square, 1e-36) * 1.02))
+                factor = TOP * jnp.exp2(code * -0.25)
+                a = jnp.round(first * factor).astype(I32)
+                b = jnp.round(second * factor).astype(I32)
+                k = p * groups + g
+                ref[where, k, 0, :] = (a << 16) | (b & 0xFFFF)
+                within = lax.broadcasted_iota(I32, code.shape, 1) % SEGMENT
+                codes = code if codes is None else jnp.where(within == k, code, codes)
+        ref[where, len(pairs) * groups, 0, :] = codes.astype(I32)
+
+    def lift(ref, where, pairs=2):
+        codes = ref[where, pairs * groups, 0, :].astype(F32)
+        within = lax.broadcasted_iota(I32, codes.shape, 1) % SEGMENT
+        values = []
+        for p in range(pairs):
+            firsts, seconds = [], []
+            for g in range(groups):
+                k = p * groups + g
+                code = jnp.dot(
+                    jnp.where(within == k, codes, 0.0).astype(BF16), segment_sum, preferred_element_type=F32
+                )
+                scale = jnp.exp2(code * 0.25) * (1.0 / TOP)
+                words = ref[where, k, 0, :]
+                firsts.append((words >> 16).astype(F32) * scale)
+                seconds.append(((words << 16) >> 16).astype(F32) * scale)
+            values.append((jnp.concatenate(firsts, axis=1), jnp.concatenate(seconds, axis=1)))
+        return values
 
     def block_moments(ref, h):
         rate = line(0)
@@ -194,16 +232,15 @@
                 pressure[lines(h, i), :] = value
             split(h, i, jnp.where(outside, value - measured[lines(h, i), :].astype(F32), 0.0))
 
-    def give(h):
+    around = [(step, y) for step in (1, 0) for y in (2, 1, 3, 0)]
+
+    def give(h, far):
         for i in range(cells):
             value = viscosity[lines(h, i), :].astype(F32) * at(result, h, i)
             put(rs_send.at[h * cells + i], value[: half // 2], value[half // 2 :])
-        for k in range(cells):
-            other = h * cells + (case + k) % cells
-
-            @pl.when(other != case)
-            def _():
-                send(rs_send.at[other], rs_got.at[case], 2, {"case": other})
+        for step, y in around if far else around[:-1]:
+            other = case_at(far, step, y)
+            send(rs_send.at[other], rs_got.at[case], 2, {"case": other})
 
     for i in range(3):
         loads[i].wait()
@@ -218,15 +255,11 @@
     for h in range(2):
         some = slice(h * half, (h + 1) * half)
         spectrum[h] = sine(h)
-        onward, backward = block_moments(spectrum, h)
-        lay(a_send, some, 0, onward)
-        lay(a_send, some, 1, backward)
+        field = block_moments(spectrum, h)
         finish(spectrum, h)
         misfit(h, False)
         result[h] = sine(h)
-        onward, backward = block_moments(result, h)
-        lay(a_send, some, 2, onward)
-        lay(a_send, some, 3, backward)
+        lay(a_send, some, field, block_moments(result, h))
     pl.semaphore_wait(barrier, cases - 1 + spaces)
     send(walls_send, walls_got, 4, solver(me))
     for o, m, i in nearby((1, 2, 3, 0)):
@@ -249,9 +282,8 @@
         return pltpu.roll(onward, 1, 0) * line(1), pltpu.roll(backward, spaces - 1, 0) * line(1)
 
     rate = line(0)
-    left, right = scan(lift(a_got, every, 0), lift(a_got, every, 1))
-    lay(b_send, every, 0, left)
-    lay(b_send, every, 1, right)
+    field, alone = lift(a_got, every)
+    left, right = scan(*field)
     quarter = cells // 2
     powers = [line(2)]
     for i in range(1, cells):
@@ -272,21 +304,21 @@
     for i in range(1, cells):
         onward = (onward + row_block(i)) * rate
         backward = (backward + row_block(cells - 1 - i)) * rate
-    left, right = scan(lift(a_got, every, 2) + onward, lift(a_got, every, 3) + backward)
-    lay(b_send, every, 2, left)
-    lay(b_send, every, 3, right)
+    lay(b_send, every, (left, right), scan(alone[0] + onward, alone[1] + backward))
     for o, m, i in nearby((1, 2, 3, 0)):
         target = place(o, m + upper_case, i)
         send(b_send.at[target], b_got.at[owned], 1, {"case": partner, "space": target})
     wait_bytes(b_got, recvs.at[1])
 
-    for h in range(2):
-        some = slice(h * half, (h + 1) * half)
-        finish(spectrum, h, lift(b_got, some, 0), lift(b_got, some, 1))
+    for far in (1, 0):
+        h = (upper_case + far) % 2
+        some = pl.ds(h * half, half)
+        first, second = lift(b_got, some)
+        finish(spectrum, h, *first)
         misfit(h, True)
         spectrum[h] = sine(h)
-        finish(spectrum, h, lift(b_got, some, 2), lift(b_got, some, 3))
-        give(h)
+        finish(spectrum, h, *second)
+        give(h, far)
     copy_out = pltpu.make_async_copy(pressure, pressure_out, out_sems.at[0])
     copy_out.start()
     rs_got[case] = rs_send[case]
@@ -299,8 +331,9 @@
         a, b = take(rs_got.at[k], groups)
         upper, lower = upper + a, lower + b
     put(ag_send, upper, lower)
-    for k in range(1, cases):
-        send(ag_send, words_out.at[case], 3, {"case": (case + k) % cases})
+    for far in (1, 0):
+        for step, y in around if far else around[:-1]:
+            send(ag_send, words_out.at[case], 3, {"case": case_at(far, step, y)})
     keep = pltpu.make_async_copy(ag_send, words_out.at[case], out_sems.at[1])
     keep.start()
     wait_bytes(rs_got.at[pl.ds(0, cases - 1)], sends.at[2])
@@ -359,7 +392,7 @@
             pltpu.VMEM(flat, F32),
             pltpu.VMEM((1, LANES), I32),
             pltpu.VMEM((1, LANES), I32),
-            *[pltpu.VMEM((spaces, 4 * groups, LANES), F32)] * 4,
+            *[pltpu.VMEM((spaces, 2 * groups + 1, 1, LANES), I32)] * 4,
             pltpu.VMEM((cases, *short), I32),
             pltpu.VMEM((cases, *short), I32),
             pltpu.VMEM(short, I32),

time: 51.1 us -> 46.5 us (0.910)
  Pallas kernels: 50.3 us -> 45.6 us
    pallas_call x1, Pallas kernels: 49.5 us -> 44.8 us  [shards(): pl.pallas_call(functools.partial(kernel, cases, cells, planes, rows), out...]
where the time goes in v5:
time: 46.5 us; the launch traced here: 46.2 us
  Pallas kernels  45.6 us (98%)
  between operations  0.64 us (1%)
    pallas_call x1, Pallas kernels, shards(): pl.pallas_call(functools.partial(kernel, cases, cells, planes, rows), out...  44.8 us

profile of v5, /device:TPU:1, one launch (start us, length us, event | category | flops | bytes accessed | tf_op | source)
XLA Modules:
  0.0 46.2 jit_solution(2185677754599143344)
XLA Ops:
  0.6 44.8 %shard_map.95 = (f32[256,256]{1,0:T(8,128)S(1)}, s32[16,18,128]{2,1,0:T(8,128)S(1)}) custom-call(bf16[256,256]{1,0:T(8,128)(2,1)} %bitcast.7, bf16[256,256]{1,0:T(8,128)(2,1)} %bitcast.8, bf16[256,256]{1,0:T(8,128)(2,1)} %bitcast.9, f32[256,256]{1,0:T(8,128)} %bitcast.6, s32[1,32]{1,0:T(1,128)} %walls_in.1, bf16[256,256]{1,0:T(8,128)(2,1)} %constant.6.clone.high_in, ...), custom_call_target="tpu_custom_call" | custom-call | tf_op jit(solution)/shard_map/pallas_call | solution.py:374
  45.4 0.8 %shard_map.96 = (f32[256,256]{1,0:T(8,128)}, f32[256,256]{1,0:T(8,128)}) custom-call(f32[256,256]{1,0:T(8,128)S(1)} %get-tuple-element.6.pressure_in, s32[16,18,128]{2,1,0:T(8,128)S(1)} %get-tuple-element.7.words), custom_call_target="tpu_custom_call" | custom-call | tf_op jit(solution)/shard_map/pallas_call | solution.py:417

commit v6 on v5

--- a/solution.py
+++ b/solution.py
@@ -80,17 +80,13 @@
            rs_send, rs_got, ag_send, in_sems, out_sems, sends, recvs):
     me = lax.axis_index("space")
     case = lax.axis_index("case")
-    inner, middle, outer = me % 2, me // 2 % MIDDLE, me // (2 * MIDDLE)
+    inner, middle, outer = me & 1, (me >> 1) & (MIDDLE - 1), lax.div(me, 2 * MIDDLE)
     half = planes // 2
     groups = rows // LANES
     spaces = 2 * OUTER * MIDDLE
-    partner = (case + cases // 2) % cases
-    upper_case = case // (cases // 2)
-    owned = (outer * MIDDLE + (middle + MIDDLE - 1 + upper_case) % MIDDLE) * 2 + inner
-
-    def solver(plane):
-        o, m, i = plane // (2 * MIDDLE), plane // 2 % MIDDLE, plane % 2
-        return {"case": partner, "space": (o * MIDDLE + (m + upper_case) % MIDDLE) * 2 + i}
+    partner = lax.rem(case + cases // 2, cases)
+    upper_case = lax.div(case, cases // 2)
+    owned = (outer * MIDDLE + ((middle + MIDDLE - 1 + upper_case) & (MIDDLE - 1))) * 2 + inner
 
     def nearby(steps):
         return [(o, m, i) for m in steps for o in (2, 1, 3, 0) for i in (1, 0)]
@@ -100,8 +96,16 @@
     def greet(device):
         pl.semaphore_signal(barrier, inc=1, device_id=device, device_id_type=MESH)
 
+    outers = [((outer + k) & (OUTER - 1)) * (2 * MIDDLE) for k in range(OUTER)]
+    middles = [((middle + k) & (MIDDLE - 1)) * 2 for k in range(MIDDLE)]
+    others = [((middle + k + upper_case) & (MIDDLE - 1)) * 2 for k in range(MIDDLE)]
+    inners = [inner, 1 - inner]
+
     def place(o, m, i):
-        return (((outer + o) % OUTER) * MIDDLE + (middle + m) % MIDDLE) * 2 + (inner + i) % 2
+        return outers[o] + middles[m] + inners[i]
+
+    def across(o, m, i):
+        return outers[o] + others[m] + inners[i]
 
     loads = [
         pltpu.make_async_copy(src, dst, in_sems.at[i])
@@ -121,18 +125,22 @@
     for load in loads[:3]:
         load.start()
     for o, m, i in nearby((1, 2, 3, 0)):
-        greet({"case": partner, "space": place(o, m + upper_case, i)})
+        greet({"case": partner, "space": across(o, m, i)})
     for load in loads[3:]:
         load.start()
     for k in range(1, cases):
-        greet({"case": (case + k) % cases})
+        greet({"case": lax.rem(case + k, cases)})
 
     def lines(h, i):
         return pl.ds(pl.multiple_of(i * planes + h * half, half), half)
 
+    halves = [upper_case, 1 - upper_case]
+    lower_bit = lax.div(case, 4) & 1
+    bits = [lower_bit * 4, 4 - lower_bit * 4]
+    columns = [(case + k) & 3 for k in range(4)]
+
     def case_at(far, step, y):
-        bit = (case // 4 + step) % 2
-        return (upper_case + far) % 2 * (cases // 2) + bit * 4 + (case + y) % 4
+        return halves[far] * (cases // 2) + bits[step] + columns[y]
 
     def split(h, i, value):
         count = value.shape[0]
@@ -222,21 +230,21 @@
             split(h, i, full * line(2))
         result[h] = sine(h)
 
-    def misfit(h, keep):
+    def misfit(f, h, keep):
         chosen = lax.broadcasted_iota(I32, (half, planes), 0) + h * half == lax.broadcasted_iota(I32, (half, planes), 1)
         first_row = jnp.sum(jnp.where(chosen, walls[...], 0), axis=1, keepdims=True)
         outside = lax.broadcasted_iota(I32, (half, rows), 1) >= first_row
         for i in range(cells):
-            value = at(result, h, i)
+            value = at(result, f, i)
             if keep:
                 pressure[lines(h, i), :] = value
-            split(h, i, jnp.where(outside, value - measured[lines(h, i), :].astype(F32), 0.0))
+            split(f, i, jnp.where(outside, value - measured[lines(h, i), :].astype(F32), 0.0))
 
     around = [(step, y) for step in (1, 0) for y in (2, 1, 3, 0)]
 
-    def give(h, far):
+    def give(f, h, far):
         for i in range(cells):
-            value = viscosity[lines(h, i), :].astype(F32) * at(result, h, i)
+            value = viscosity[lines(h, i), :].astype(F32) * at(result, f, i)
             put(rs_send.at[h * cells + i], value[: half // 2], value[half // 2 :])
         for step, y in around if far else around[:-1]:
             other = case_at(far, step, y)
@@ -244,27 +252,27 @@
 
     for i in range(3):
         loads[i].wait()
-    for h in range(2):
+    for f in range(2):
         for i in range(cells):
-            part = lines(h, i)
-            split(h, i, forcing[part, :].astype(F32) + viscosity[part, :].astype(F32) * correction[part, :])
+            part = lines(halves[1 - f], i)
+            split(f, i, forcing[part, :].astype(F32) + viscosity[part, :].astype(F32) * correction[part, :])
     for i in range(3, 8):
         loads[i].wait()
     walls_send[...] = jnp.zeros_like(walls_send)
     walls_send[:, 0:planes] = walls[...]
-    for h in range(2):
-        some = slice(h * half, (h + 1) * half)
-        spectrum[h] = sine(h)
-        field = block_moments(spectrum, h)
-        finish(spectrum, h)
-        misfit(h, False)
-        result[h] = sine(h)
-        lay(a_send, some, field, block_moments(result, h))
+    for f in range(2):
+        h = halves[1 - f]
+        spectrum[f] = sine(f)
+        field = block_moments(spectrum, f)
+        finish(spectrum, f)
+        misfit(f, h, False)
+        result[f] = sine(f)
+        lay(a_send, pl.ds(h * half, half), field, block_moments(result, f))
     pl.semaphore_wait(barrier, cases - 1 + spaces)
-    send(walls_send, walls_got, 4, solver(me))
+    send(walls_send, walls_got, 4, {"case": partner, "space": across(0, 0, 0)})
     for o, m, i in nearby((1, 2, 3, 0)):
         plane = place(o, m, i)
-        send(a_send.at[plane], a_got.at[me], 0, solver(plane))
+        send(a_send.at[plane], a_got.at[me], 0, {"case": partner, "space": across(o, m, i)})
 
     wait_bytes(walls_got, recvs.at[4])
     chosen = lax.broadcasted_iota(I32, walls_got.shape, 1) == owned
@@ -306,19 +314,21 @@
         backward = (backward + row_block(cells - 1 - i)) * rate
     lay(b_send, every, (left, right), scan(alone[0] + onward, alone[1] + backward))
     for o, m, i in nearby((1, 2, 3, 0)):
-        target = place(o, m + upper_case, i)
+        target = across(o, m, i)
         send(b_send.at[target], b_got.at[owned], 1, {"case": partner, "space": target})
     wait_bytes(b_got, recvs.at[1])
 
-    for far in (1, 0):
-        h = (upper_case + far) % 2
-        some = pl.ds(h * half, half)
-        first, second = lift(b_got, some)
-        finish(spectrum, h, *first)
-        misfit(h, True)
-        spectrum[h] = sine(h)
-        finish(spectrum, h, *second)
-        give(h, far)
+    rows_back = [lift(b_got, pl.ds(halves[1 - f] * half, half)) for f in range(2)]
+    for f in range(2):
+        finish(spectrum, f, *rows_back[f][0])
+    for f in range(2):
+        misfit(f, halves[1 - f], True)
+    for f in range(2):
+        spectrum[f] = sine(f)
+    for f in range(2):
+        finish(spectrum, f, *rows_back[f][1])
+    for f in range(2):
+        give(f, halves[1 - f], 1 - f)
     copy_out = pltpu.make_async_copy(pressure, pressure_out, out_sems.at[0])
     copy_out.start()
     rs_got[case] = rs_send[case]
@@ -362,7 +372,7 @@
 def shards(forcing, viscosity, measured, correction, wall_rows):
     cells, planes, rows = correction.shape
     spaces, cases = lax.axis_size("space"), lax.axis_size("case")
-    assert spaces == 2 * OUTER * MIDDLE and cases == 2 * cells
+    assert spaces == 2 * OUTER * MIDDLE and cases == 2 * cells == 16
     high, low = sine_tables(rows)
     modes = mode_table(rows, cells, cells * spaces, 1.0 / (2.0 * cells))
     flat = (cells * planes, rows)

time: 46.5 us -> 46.5 us (level)
  no operation moved by 1% of the time
where the time goes in v6:
time: 46.5 us; the launch traced here: 46.3 us
  Pallas kernels  45.6 us (98%)
  between operations  0.64 us (1%)
    pallas_call x1, Pallas kernels, shards(): pl.pallas_call(functools.partial(kernel, cases, cells, planes, rows), out...  44.8 us

profile of v6, /device:TPU:1, one launch (start us, length us, event | category | flops | bytes accessed | tf_op | source)
XLA Modules:
  0.0 46.3 jit_solution(8484223627302481064)
XLA Ops:
  0.6 44.8 %shard_map.95 = (f32[256,256]{1,0:T(8,128)S(1)}, s32[16,18,128]{2,1,0:T(8,128)S(1)}) custom-call(bf16[256,256]{1,0:T(8,128)(2,1)} %bitcast.7, bf16[256,256]{1,0:T(8,128)(2,1)} %bitcast.8, bf16[256,256]{1,0:T(8,128)(2,1)} %bitcast.9, f32[256,256]{1,0:T(8,128)} %bitcast.6, s32[1,32]{1,0:T(1,128)} %walls_in.1, bf16[256,256]{1,0:T(8,128)(2,1)} %constant.6.clone.high_in, ...), custom_call_target="tpu_custom_call" | custom-call | tf_op jit(solution)/shard_map/pallas_call | solution.py:384
  45.5 0.8 %shard_map.96 = (f32[256,256]{1,0:T(8,128)}, f32[256,256]{1,0:T(8,128)}) custom-call(f32[256,256]{1,0:T(8,128)S(1)} %get-tuple-element.6.pressure_in, s32[16,18,128]{2,1,0:T(8,128)S(1)} %get-tuple-element.7.words), custom_call_target="tpu_custom_call" | custom-call | tf_op jit(solution)/shard_map/pallas_call | solution.py:427

commit v7 on v5

--- a/solution.py
+++ b/solution.py
@@ -162,9 +162,8 @@
 
     segment_sum = (segments(0) == segments(1)).astype(BF16)
 
-    def lay(ref, where, *pairs):
-        codes = None
-        for p, pair in enumerate(pairs):
+    def lay(ref, where, *pairs, start=0, codes=None):
+        for p, pair in enumerate(pairs, start):
             for g in range(groups):
                 first, second = (value[:, g * LANES : (g + 1) * LANES] for value in pair)
                 square = jnp.dot(
@@ -178,7 +177,9 @@
                 ref[where, k, 0, :] = (a << 16) | (b & 0xFFFF)
                 within = lax.broadcasted_iota(I32, code.shape, 1) % SEGMENT
                 codes = code if codes is None else jnp.where(within == k, code, codes)
-        ref[where, len(pairs) * groups, 0, :] = codes.astype(I32)
+        if p == 1:
+            ref[where, 2 * groups, 0, :] = codes.astype(I32)
+        return codes
 
     def lift(ref, where, pairs=2):
         codes = ref[where, pairs * groups, 0, :].astype(F32)
@@ -284,6 +285,7 @@
     rate = line(0)
     field, alone = lift(a_got, every)
     left, right = scan(*field)
+    codes = lay(b_send, every, (left, right))
     quarter = cells // 2
     powers = [line(2)]
     for i in range(1, cells):
@@ -304,7 +306,7 @@
     for i in range(1, cells):
         onward = (onward + row_block(i)) * rate
         backward = (backward + row_block(cells - 1 - i)) * rate
-    lay(b_send, every, (left, right), scan(alone[0] + onward, alone[1] + backward))
+    lay(b_send, every, scan(alone[0] + onward, alone[1] + backward), start=1, codes=codes)
     for o, m, i in nearby((1, 2, 3, 0)):
         target = place(o, m + upper_case, i)
         send(b_send.at[target], b_got.at[owned], 1, {"case": partner, "space": target})

time: 46.5 us -> 46.5 us (level)
  no operation moved by 1% of the time
where the time goes in v7:
time: 46.5 us; the launch traced here: 46.2 us
  Pallas kernels  45.5 us (98%)
  between operations  0.64 us (1%)
    pallas_call x1, Pallas kernels, shards(): pl.pallas_call(functools.partial(kernel, cases, cells, planes, rows), out...  44.7 us

profile of v7, /device:TPU:1, one launch (start us, length us, event | category | flops | bytes accessed | tf_op | source)
XLA Modules:
  0.0 46.2 jit_solution(12041542080333961415)
XLA Ops:
  0.6 44.7 %shard_map.95 = (f32[256,256]{1,0:T(8,128)S(1)}, s32[16,18,128]{2,1,0:T(8,128)S(1)}) custom-call(bf16[256,256]{1,0:T(8,128)(2,1)} %bitcast.7, bf16[256,256]{1,0:T(8,128)(2,1)} %bitcast.8, bf16[256,256]{1,0:T(8,128)(2,1)} %bitcast.9, f32[256,256]{1,0:T(8,128)} %bitcast.6, s32[1,32]{1,0:T(1,128)} %walls_in.1, bf16[256,256]{1,0:T(8,128)(2,1)} %constant.6.clone.high_in, ...), custom_call_target="tpu_custom_call" | custom-call | tf_op jit(solution)/shard_map/pallas_call | solution.py:376
  45.4 0.8 %shard_map.96 = (f32[256,256]{1,0:T(8,128)}, f32[256,256]{1,0:T(8,128)}) custom-call(f32[256,256]{1,0:T(8,128)S(1)} %get-tuple-element.6.pressure_in, s32[16,18,128]{2,1,0:T(8,128)S(1)} %get-tuple-element.7.words), custom_call_target="tpu_custom_call" | custom-call | tf_op jit(solution)/shard_map/pallas_call | solution.py:419
